TPU v7x, 128 devices: a whole 4x4x4 slice. The times are simulated.
128 devices in a mesh: dp: 8 (over x_hi, z), tensor: 16 (over x_lo, y, core).
Axes of the slice: x: 4 (x_hi: 2, x_lo: 2; x = x_hi * 2 + x_lo), y: 4, z: 4, core: 2. Of those that a mesh axis runs over, the one named last changes fastest.
Arguments:
- dense_hidden: bfloat16 [2048, 9216], P('dp', 'tensor'), may hold values from -6 to 6
- dense_down: bfloat16 [9216, 3584], P('tensor', 'dp'), may hold values from -0.0625 to 0.0625
- residual: bfloat16 [2048, 3584], P(('dp', 'tensor')), may hold values from -6 to 6
- norm_gain: bfloat16 [3584], replicated, may hold values from 0.099609375 to 1.8984375
- expert_ids: int32 [2048, 8], P(('dp', 'tensor')), may hold values from 0 to 127, all different within a row; in each aligned block of 16 rows (0 to 15, 16 to 31, ...) at most 2 rows name the same one
- route_weights: float32 [2048, 8], P(('dp', 'tensor')), may hold values from 0.05 to 0.5
- w_gate: bfloat16 [128, 3584, 1024], P(('dp', 'tensor')), may hold values from -0.09375 to 0.09375
- w_up: bfloat16 [128, 3584, 1024], P(('dp', 'tensor')), may hold values from -0.09375 to 0.09375
- w_down: bfloat16 [128, 1024, 3584], P(('dp', 'tensor')), may hold values from -0.1875 to 0.1875
- out_cotangent: bfloat16 [2048, 3584], P(('dp', 'tensor')), may hold values from -6 to 6
Outputs:
- moe_out: bfloat16 [2048, 3584], P(('dp', 'tensor'))
- grad_stream: bfloat16 [2048, 3584], P(('dp', 'tensor'))
- grad_hidden: bfloat16 [2048, 9216], P('dp', 'tensor')
Inputs may be any that keep to these rules, and one draw needn't show every extreme that they name: `expert_ids`: each row names 8 different experts. Among the 16 rows of one aligned block no expert is named more than 2 times, a bound that some block reaches.
All inputs are finite; a program needn't handle non-finite values.
Results may differ from a plain program's by a relative error of at most 0.012.
Values may be sent and summed in bfloat16 or wider, within the bound.
A program may use at most 128 MiB of HBM per device.

v0:
```python
import jax
import jax.numpy as jnp
from jax import lax
from jax.sharding import PartitionSpec as P


def to_experts(rows):
    return lax.all_to_all(rows, ("dp", "tensor"), split_axis=1, concat_axis=1, tiled=True)


def to_tokens(rows):
    return lax.all_to_all(rows, ("dp", "tensor"), split_axis=1, concat_axis=1, tiled=True)


def body(
    dense_hidden,
    dense_down,
    residual,
    norm_gain,
    expert_ids,
    route_weights,
    w_gate,
    w_up,
    w_down,
    out_cotangent,
):
    tok_rows = residual.shape[0]
    model_width = residual.shape[1]
    top_count = expert_ids.shape[1]
    devices = lax.axis_size(("dp", "tensor"))
    capacity = max(2, 2 * tok_rows * top_count // devices)
    contract = (((1,), (1,)), ((), ()))
    down_full = lax.all_gather(dense_down, "dp", axis=1, tiled=True)
    dense_out = lax.psum_scatter(
        jnp.dot(dense_hidden, down_full, preferred_element_type=jnp.float32),
        "tensor",
        scatter_dimension=0,
        tiled=True,
    )
    stream = (residual.astype(jnp.float32) + dense_out).astype(jnp.bfloat16)
    stream_f = stream.astype(jnp.float32)
    inverse = lax.rsqrt(jnp.mean(stream_f * stream_f, axis=-1, keepdims=True) + 1e-06)
    gain_f = norm_gain.astype(jnp.float32)
    normed = (stream_f * inverse * gain_f).astype(jnp.bfloat16)
    expert_iota = jnp.arange(devices, dtype=jnp.int32)
    onehot = (
        (expert_ids[:, :, None] == expert_iota[None, None, :])
        .astype(jnp.int32)
        .reshape(tok_rows * top_count, devices)
    )
    running = jnp.cumsum(onehot, axis=0) - onehot
    slot_index = jnp.sum(running * onehot, axis=1).reshape(tok_rows, top_count)
    spread_rows = jnp.broadcast_to(normed[:, None, :], (tok_rows, top_count, model_width))
    send = (
        jnp.zeros((capacity, devices, model_width), jnp.bfloat16)
        .at[slot_index, expert_ids]
        .set(spread_rows)
    )
    cotangent = out_cotangent.astype(jnp.float32)
    grad_rows = (route_weights[:, :, None] * cotangent[:, None, :]).astype(jnp.bfloat16)
    grad_send = (
        jnp.zeros((capacity, devices, model_width), jnp.bfloat16)
        .at[slot_index, expert_ids]
        .set(grad_rows)
    )
    gate_w = w_gate[0]
    up_w = w_up[0]
    down_w = w_down[0]
    arrived = to_experts(send)
    gate_pre = jnp.einsum("cnd,df->cnf", arrived, gate_w, preferred_element_type=jnp.float32)
    up_pre = jnp.einsum("cnd,df->cnf", arrived, up_w, preferred_element_type=jnp.float32)
    act = (jax.nn.silu(gate_pre) * up_pre).astype(jnp.bfloat16)
    expert_out = jnp.einsum("cnf,fd->cnd", act, down_w, preferred_element_type=jnp.float32).astype(
        jnp.bfloat16
    )
    expert_out, gate_pre, up_pre = (expert_out, gate_pre, up_pre)
    returned = to_tokens(expert_out)
    grad_arrived = to_experts(grad_send)
    grad_act = jnp.einsum("cnd,fd->cnf", grad_arrived, down_w, preferred_element_type=jnp.float32)
    sigmoid_g = jax.nn.sigmoid(gate_pre)
    silu_gate = gate_pre * sigmoid_g
    grad_gate = (grad_act * up_pre * sigmoid_g * (1.0 + gate_pre * (1.0 - sigmoid_g))).astype(
        jnp.bfloat16
    )
    grad_up = (grad_act * silu_gate).astype(jnp.bfloat16)
    grad_in = jnp.einsum("cnf,df->cnd", grad_gate, gate_w, preferred_element_type=jnp.float32)
    grad_in = grad_in + jnp.einsum("cnf,df->cnd", grad_up, up_w, preferred_element_type=jnp.float32)
    grad_back = to_tokens(grad_in.astype(jnp.bfloat16))
    picked = returned[slot_index, expert_ids].astype(jnp.float32)
    moe_out = (stream_f + jnp.sum(route_weights[:, :, None] * picked, axis=1)).astype(jnp.bfloat16)
    grad_normed = jnp.sum(grad_back[slot_index, expert_ids].astype(jnp.float32), axis=1)
    unit = stream_f * inverse
    scaled = grad_normed * gain_f
    grad_f = cotangent + inverse * (scaled - unit * jnp.mean(scaled * unit, axis=-1, keepdims=True))
    grad_stream = grad_f.astype(jnp.bfloat16)
    grad_hidden = lax.dot_general(
        lax.all_gather(grad_stream, "tensor", axis=0, tiled=True),
        down_full,
        contract,
        preferred_element_type=jnp.float32,
    ).astype(jnp.bfloat16)
    return (moe_out, grad_stream, grad_hidden)


def solution(mesh):
    placed = (
        P("dp", "tensor"),
        P("tensor", "dp"),
        P(("dp", "tensor"), None),
        P(),
        P(("dp", "tensor"), None),
        P(("dp", "tensor"), None),
        P(("dp", "tensor"), None, None),
        P(("dp", "tensor"), None, None),
        P(("dp", "tensor"), None, None),
        P(("dp", "tensor"), None),
    )
    return jax.shard_map(
        body,
        mesh=mesh,
        in_specs=placed,
        out_specs=(P(("dp", "tensor"), None), P(("dp", "tensor"), None), P("dp", "tensor")),
        check_vma=False,
    )
```

profile of v0, /device:TPU:33, one launch (start us, length us, event | category | flops | bytes accessed | tf_op | source)
XLA Modules:
  0.0 409.2 jit_solution(6748219288682191502)
XLA Ops:
  7.2 0.0 copy-start
  7.2 0.0 all-gather.3.cloned.1.call-start
  7.2 0.7 all-gather.3.cloned.1.call-update
  7.9 0.0 reduce-scatter.2.cloned.1.call-start
  8.0 77.5 %all-gather.3.cloned.1.call-done = bf16[576,3584]{0,1:T(8,128)(2,1)} async-done(((bf16[576,448]{0,1:T(8,128)(2,1)}), bf16[576,3584]{0,1:T(8,128)(2,1)}) %all-gather.3.cloned.1.call-update) | async-done | bytes 4128784 | tf_op jit(solution)/shard_map/all_gather | solution.py:33
  85.4 0.0 copy-done
  85.4 5.8 %fusion.49 = f32[256,3584]{1,0:T(8,128)} fusion(bf16[256,576]{0,1:T(8,128)(2,1)S(1)} %copy-done, bf16[576,3584]{0,1:T(8,128)(2,1)} %all-gather.3.cloned.1.call-done), kind=kOutput, calls=%fused_computation.68 | convolution fusion | flops 1056964608 | bytes 8093696 | tf_op jit(solution)/shard_map/dot_general | solution.py:35
  91.2 0.0 reduce-scatter.2.cloned.1.call-update
  91.2 0.7 copy-done.5
  91.9 0.1 copy.33
  92.0 0.1 copy.35
  92.0 0.1 eq.16
  92.1 0.0 copy-done.6
  92.1 0.1 fusion.41
  92.2 0.2 reduce_window_sum.11
  92.4 0.2 select_reduce_fusion
  92.6 0.1 reshape.57
  92.7 0.1 reshape.70
  92.8 60.5 %reduce-scatter.2.cloned.1.call-done = f32[16,3584]{1,0:T(8,128)} async-done(((f32[256,3584]{1,0:T(8,128)}), f32[16,3584]{1,0:T(8,128)}) %reduce-scatter.2.cloned.1.call-update) | async-done | bytes 229392 | tf_op jit(solution)/shard_map/reduce_scatter | solution.py:34
  153.3 0.0 copy-done.4
  153.3 1.1 fusion.37
  154.4 0.1 fusion.31
  154.5 0.1 broadcast_bitcast_fusion
  154.6 0.1 broadcast.63.clone
  154.7 17.7 %scatter_fusion = bf16[2,128,3584]{2,1,0:T(8,128)(2,1)S(1)} fusion(bf16[2,128,3584]{2,1,0:T(8,128)(2,1)S(1)} %broadcast.63.clone, s32[128]{0:T(128)S(1)} %reshape.70, bf16[128,3584]{1,0:T(8,128)(2,1)S(1)} %broadcast_bitcast_fusion), kind=kCustom, calls=%fused_computation.2 | custom fusion | bytes 2753536 | tf_op jit(solution)/shard_map/scatter | solution.py:57
  172.4 1.9 copy.36
  174.3 0.0 slice-start.2
  174.3 37.9 %all_to_all.20 = bf16[2,128,3584]{2,0,1:T(2,128)(2,1)S(1)} all-to-all(bf16[2,128,3584]{2,0,1:T(2,128)(2,1)S(1)} %copy.36), channel_id=1, replica_groups=mesh['dp'=8,'tensor'=16] {'dp','tensor'}, dimensions={1} | all-to-all | bytes 3670016 | tf_op jit(solution)/shard_map/all_to_all | solution.py:8
  212.2 5.3 %fusion.10 = f32[2,128,1024]{2,1,0:T(8,128)S(1)} fusion(bf16[1,3584,1024]{2,1,0:T(8,128)(2,1)} %param.16, bf16[2,128,3584]{2,0,1:T(2,128)(2,1)S(1)} %all_to_all.20), kind=kOutput, calls=%fused_computation.14 | convolution fusion | flops 1879048192 | bytes 10223616 | tf_op jit(solution)/shard_map/cnd,df->cnf/dot_general | solution.py:70
  217.6 0.0 slice-start.1
  217.6 2.1 fusion.6
  219.7 0.2 slice-done.1
  219.8 2.1 fusion.15
  222.0 3.1 copy.39
  225.1 6.3 %all-to-all-start.1 = ((bf16[2,128,3584]{2,0,1:T(2,128)(2,1)}), bf16[2,128,3584]{2,0,1:T(2,128)(2,1)}, u32[]{:S(2)}, u32[]{:S(2)}) async-start(bf16[2,128,3584]{2,0,1:T(2,128)(2,1)} %copy.39), calls=%async_computation.2 | async-start | bytes 3670016 | tf_op jit(solution)/shard_map/all_to_all | solution.py:12
  231.4 0.2 all-gather.5.cloned.1.call-start
  231.7 0.0 copy-done.7
  231.7 0.1 copy.32
  231.8 0.1 reshape.58
  231.9 26.3 %all-to-all-done.1 = bf16[2,128,3584]{2,0,1:T(2,128)(2,1)} async-done(((bf16[2,128,3584]{2,0,1:T(2,128)(2,1)}), bf16[2,128,3584]{2,0,1:T(2,128)(2,1)}, u32[]{:S(2)}, u32[]{:S(2)}) %all-to-all-start.1) | async-done | bytes 1835040 | tf_op jit(solution)/shard_map/all_to_all | solution.py:12
  258.2 1.7 copy.40
  259.9 3.6 gather_fusion
  263.5 1.3 fusion.26
  264.8 0.1 broadcast.63
  264.9 1.1 copy-done.2
  265.9 17.7 %scatter_fusion.1 = bf16[2,128,3584]{2,1,0:T(8,128)(2,1)S(1)} fusion(bf16[2,128,3584]{2,1,0:T(8,128)(2,1)S(1)} %broadcast.63, s32[128]{0:T(128)S(1)} %reshape.70, bf16[128,3584]{1,0:T(8,128)(2,1)S(1)} %copy-done.2), kind=kCustom, calls=%fused_computation.3 | custom fusion | bytes 2753536 | tf_op jit(solution)/shard_map/scatter | solution.py:64
  283.7 1.9 copy.41
  285.6 0.0 slice-start.4
  285.6 0.0 slice-start.6
  285.6 32.1 %all_to_all.21 = bf16[2,128,3584]{2,0,1:T(2,128)(2,1)S(1)} all-to-all(bf16[2,128,3584]{2,0,1:T(2,128)(2,1)S(1)} %copy.41), channel_id=1, replica_groups=mesh['dp'=8,'tensor'=16] {'dp','tensor'}, dimensions={1} | all-to-all | bytes 3670016 | tf_op jit(solution)/shard_map/all_to_all | solution.py:8
  317.7 5.3 %fusion = f32[2,128,1024]{2,1,0:T(8,128)S(1)} fusion(bf16[1,1024,3584]{2,1,0:T(8,128)(2,1)} %param.18, bf16[2,128,3584]{2,0,1:T(2,128)(2,1)S(1)} %all_to_all.21), kind=kOutput, calls=%fused_computation.4 | convolution fusion | flops 1879048192 | bytes 10223616 | tf_op jit(solution)/shard_map/cnd,fd->cnf/dot_general | solution.py:79
  323.1 2.1 fusion.4
  325.3 2.3 fusion.18
  327.6 1.9 copy.43
  329.5 31.9 %all_to_all.22 = bf16[2,128,3584]{2,0,1:T(2,128)(2,1)S(1)} all-to-all(bf16[2,128,3584]{2,0,1:T(2,128)(2,1)S(1)} %copy.43), channel_id=1, replica_groups=mesh['dp'=8,'tensor'=16] {'dp','tensor'}, dimensions={1} | all-to-all | bytes 3670016 | tf_op jit(solution)/shard_map/all_to_all | solution.py:12
  361.4 0.2 copy.44
  361.6 3.6 gather_fusion.1
  365.1 0.6 convert_reduce_fusion
  365.7 0.2 fusion.32
  366.0 0.8 fusion.36
  366.7 0.0 all-gather.5.cloned.1.call-update
  366.8 30.2 %all-gather.5.cloned.1.call-done = bf16[256,3584]{1,0:T(8,128)(2,1)} async-done(((bf16[16,3584]{1,0:T(8,128)(2,1)}), bf16[256,3584]{1,0:T(8,128)(2,1)}) %all-gather.5.cloned.1.call-update) | async-done | bytes 1835024 | tf_op jit(solution)/shard_map/all_gather | solution.py:97
  397.0 5.4 %convolution_convert_fusion = bf16[256,576]{0,1:T(8,128)(2,1)} fusion(bf16[256,3584]{1,0:T(8,128)(2,1)} %all-gather.5.cloned.1.call-done, bf16[576,3584]{0,1:T(8,128)(2,1)} %all-gather.3.cloned.1.call-done), kind=kOutput, calls=%fused_computation.26 | convolution fusion | flops 1057112064 | bytes 6258688 | tf_op jit(solution)/shard_map/dot_general | solution.py:96
  402.4 0.0 copy-done.1
  (37 shorter events, 0.1 us)
Async XLA Ops:
  7.2 78.3 %copy-start = (bf16[256,576]{0,1:T(8,128)(2,1)S(1)}, bf16[256,576]{0,1:T(8,128)(2,1)}, u32[]{:S(2)}) copy-start(bf16[256,576]{0,1:T(8,128)(2,1)} %param.10) | copy-start | bytes 884740
  7.2 78.2 %all-gather.3.cloned.1.call-start = ((), (), s32[]{:S(2)}) async-start(), calls=%async_computation.5 | async-start | bytes 5160960 | tf_op jit(solution)/shard_map/all_gather | solution.py:33
  7.9 145.4 %reduce-scatter.2.cloned.1.call-start = ((), (), s32[]{:S(2)}) async-start(), calls=%async_computation.6 | async-start | bytes 3899392 | tf_op jit(solution)/shard_map/reduce_scatter | solution.py:34
  91.2 0.7 copy-start.5
  91.2 0.9 copy-start.6
  91.2 62.1 %copy-start.4 = (bf16[16,3584]{1,0:T(8,128)(2,1)S(1)}, bf16[16,3584]{1,0:T(8,128)(2,1)}, u32[]{:S(2)}) copy-start(bf16[16,3584]{1,0:T(8,128)(2,1)} %param.12) | copy-start | bytes 344068
  174.3 43.2 %slice-start.2 = ((s8[7340032]{0:T(1024)(128)(4,1)}), s8[4194304]{0:T(1024)(128)(4,1)S(1)}, s32[]{:S(2)}) async-start(s8[7340032]{0:T(1024)(128)(4,1)} %bitcast.48), calls=%async_computation.10 | async-start | bytes 8388608
  212.2 5.3 %slice-start.3 = ((s8[7340032]{0:T(1024)(128)(4,1)}), s8[3145728]{0:T(1024)(128)(4,1)S(1)}, s32[]{:S(2)}) async-start(s8[7340032]{0:T(1024)(128)(4,1)} %bitcast.48), calls=%async_computation.11 | async-start | bytes 6291456
  212.2 7.4 %slice-start = ((s8[7340032]{0:T(1024)(128)(4,1)}), s8[4194304]{0:T(1024)(128)(4,1)S(1)}, s32[]{:S(2)}) async-start(s8[7340032]{0:T(1024)(128)(4,1)} %bitcast.46), calls=%async_computation.8 | async-start | bytes 8388608
  217.6 2.1 copy-start.8
  217.6 2.3 slice-start.1
  219.8 2.1 copy-start.10
  225.1 6.6 %copy-start.7 = (f32[16,8]{0,1:T(8,128)S(1)}, f32[16,8]{0,1:T(8,128)}, u32[]{:S(2)}) copy-start(f32[16,8]{0,1:T(8,128)} %param.15) | copy-start | bytes 1540
  225.1 6.7 %copy-start.3 = (bf16[16,3584]{1,0:T(8,128)(2,1)S(1)}, bf16[16,3584]{1,0:T(8,128)(2,1)}, u32[]{:S(2)}) copy-start(bf16[16,3584]{1,0:T(8,128)(2,1)} %param.19) | copy-start | bytes 344068
  225.1 33.1 %all-to-all-start.1 = ((bf16[2,128,3584]{2,0,1:T(2,128)(2,1)}), bf16[2,128,3584]{2,0,1:T(2,128)(2,1)}, u32[]{:S(2)}, u32[]{:S(2)}) async-start(bf16[2,128,3584]{2,0,1:T(2,128)(2,1)} %copy.39), calls=%async_computation.2 | async-start | bytes 3670016 | tf_op jit(solution)/shard_map/all_to_all | solution.py:12
  231.4 165.5 %all-gather.5.cloned.1.call-start = ((), (), s32[]{:S(2)}) async-start(), calls=%async_computation.7 | async-start | bytes 1949696 | tf_op jit(solution)/shard_map/all_gather | solution.py:97
  264.8 1.2 copy-start.2
  285.6 37.5 %slice-start.4 = ((s8[7340032]{0:T(1024)(128)(4,1)}), s8[4194304]{0:T(1024)(128)(4,1)S(1)}, s32[]{:S(2)}) async-start(s8[7340032]{0:T(1024)(128)(4,1)} %bitcast.50), calls=%async_computation.12 | async-start | bytes 8388608
  285.6 39.7 %slice-start.6 = ((s8[7340032]{0:T(1024)(128)(4,1)}), s8[4194304]{0:T(1024)(128)(4,1)S(1)}, s32[]{:S(2)}) async-start(s8[7340032]{0:T(1024)(128)(4,1)} %bitcast.52), calls=%async_computation.14 | async-start | bytes 8388608
  317.7 5.3 %slice-start.5 = ((s8[7340032]{0:T(1024)(128)(4,1)}), s8[3145728]{0:T(1024)(128)(4,1)S(1)}, s32[]{:S(2)}) async-start(s8[7340032]{0:T(1024)(128)(4,1)} %bitcast.50), calls=%async_computation.13 | async-start | bytes 6291456
  317.7 5.4 %copy-start.9 = (f32[2,128,1024]{2,1,0:T(8,128)S(1)}, f32[2,128,1024]{2,1,0:T(8,128)}, u32[]{:S(2)}) copy-start(f32[2,128,1024]{2,1,0:T(8,128)} %copy-done.8) | copy-start | bytes 3145732
  317.7 7.5 %slice-start.7 = ((s8[7340032]{0:T(1024)(128)(4,1)}), s8[3145728]{0:T(1024)(128)(4,1)S(1)}, s32[]{:S(2)}) async-start(s8[7340032]{0:T(1024)(128)(4,1)} %bitcast.52), calls=%async_computation.15 | async-start | bytes 6291456
  323.1 2.2 copy-start.11
  397.0 5.4 %copy-start.1 = (bf16[256,576]{0,1:T(8,128)(2,1)S(1)}, bf16[256,576]{0,1:T(8,128)(2,1)}, u32[]{:S(2)}) copy-start(bf16[256,576]{0,1:T(8,128)(2,1)} %param.10) | copy-start | bytes 884740
Sparse Core Ops, SparseCore 0:
  10.3 75.0 all-gather.2
  91.4 61.8 reduce-scatter.1
  366.9 30.0 all-gather.4
where the time goes:
time: 416 us; the launch traced here: 409 us
  waiting for transfers between devices  195 us (47%)
  blocking collectives  102 us (25%)
  local copies, waits for them, and re-layouts  56.1 us (13%)
  matrix products  30.4 us (7%)
  between operations  14.4 us (3%)
  starting transfers between devices  6.63 us (2%)
  other arithmetic  4.59 us (1%)
    all_gather x1, waiting for transfers between devices, body(): down_full = lax.all_gather(dense_down, 'dp', axis=1, tiled=True)  77.5 us
    all_to_all x2, blocking collectives, to_experts(): lax.all_to_all(rows, ('dp', 'tensor'), split_axis=1, concat_axis=1, tiled...  70 us
    reduce_scatter x1, waiting for transfers between devices, body(): lax.psum_scatter(jnp.dot(dense_hidden, down_full, preferred_element_type=...  60.5 us
    all_to_all x1, blocking collectives, to_tokens(): lax.all_to_all(rows, ('dp', 'tensor'), split_axis=1, concat_axis=1, tiled...  31.9 us
    all_gather x1, waiting for transfers between devices, body(): lax.all_gather(grad_stream, 'tensor', axis=0, tiled=True)  30.2 us
    all_to_all x1, waiting for transfers between devices, to_tokens(): lax.all_to_all(rows, ('dp', 'tensor'), split_axis=1, concat_axis=1, tiled...  26.3 us
    scatter x2, local copies, waits for them, and re-layouts, body(): send = jnp.zeros((capacity, devices, model_width), jnp.bfloat16).at[slot_...  19.6 us
    scatter x2, local copies, waits for them, and re-layouts, body(): grad_send = jnp.zeros((capacity, devices, model_width), jnp.bfloat16).at[...  19.6 us
  transfers between devices with their start and end apart: 4, of which 4 were waited for; matrix products, arithmetic and copies ran while one was open for 0% of the time, Pallas kernels for 0%

commit v1 on v0

v1 whole, which is shorter than its diff:
```python
import jax
import jax.numpy as jnp
from jax import lax
from jax.experimental import pallas as pl
from jax.experimental.pallas import tpu as pltpu
from jax.sharding import PartitionSpec as P

MESH = pl.DeviceIdType.MESH
BF = jnp.bfloat16
F32 = jnp.float32
CHIPS = 64
ROWS = 16
NT = (((1,), (1,)), ((), ()))


def mm(a, b):
    return jnp.dot(a, b, preferred_element_type=F32)


def mm_t(a, b):
    return lax.dot_general(a, b, NT, preferred_element_type=F32)


def landed(ref, sem):
    pltpu.make_async_copy(ref, ref, sem).wait()


def kernel(
    hid_h, down_h, res, gain, cot, key_in, wt_in, wg_h, wu_h, wd_h,
    moe_o, gs_o, gh_o,
    hid, down, wg, wu, wd,
    cot2, key2, wt2, nrm2,
    m01, mg, c01, cw, perm, perm_t, cn, cg,
    buf_a, garr, buf_b, narr, hret, eret,
    xin, gact, act, gg, gu, zin,
    pf, psend, prec, rs_send, rs_recv, stream,
    acc, pax, prx, gs_all,
    loc, ex_s, ex_r, ag_s, ag_r, ps_s, ps_r, rs_s, rs_r,
    ga_s, ga_r, na_s, na_r, ha_s, ha_r, ea_s, ea_r, px_s, px_r, gs_s, gs_r, fw_s, fw_r,
):
    width = res.shape[1]
    quarter = width // 4
    half = quarter // 2
    dp = lax.axis_index("dp")
    tn = lax.axis_index("tensor")
    c = tn % 2
    tc = tn // 2
    chip = dp * 8 + tc
    z, y = dp % 4, tc % 4
    x = (dp // 4) * 2 + tc // 4
    partner = (dp, tc * 2 + 1 - c)

    def peer(i):
        x2 = (x + i % 4) % 4
        y2 = (y + (i // 4) % 4) % 4
        z2 = (z + i // 16) % 4
        return (x2 // 2) * 4 + z2, (x2 % 2) * 4 + y2

    def send(src, dst, s_sem, r_sem, device):
        copy = pltpu.make_async_remote_copy(
            src_ref=src, dst_ref=dst, send_sem=s_sem, recv_sem=r_sem,
            device_id=device, device_id_type=MESH,
        )
        copy.start()
        return copy

    pltpu.make_async_copy(down_h, down.at[dp], ag_r.at[dp]).start()
    load_hid = pltpu.make_async_copy(hid_h, hid, loc.at[0])
    load_hid.start()
    load_wd = pltpu.make_async_copy(wd_h, wd, loc.at[1])
    load_wg = pltpu.make_async_copy(wg_h, wg, loc.at[2])
    load_wu = pltpu.make_async_copy(wu_h, wu, loc.at[3])
    load_wd.start()
    load_wg.start()
    load_wu.start()

    barrier = pltpu.get_barrier_semaphore()

    def greet(i, carry):
        d2, t2 = peer(i)
        pl.semaphore_signal(barrier, inc=1, device_id=(d2, t2 * 2 + c), device_id_type=MESH)
        return carry

    lax.fori_loop(1, CHIPS, greet, 0)
    pl.semaphore_signal(barrier, inc=1, device_id=partner, device_id_type=MESH)
    pl.semaphore_wait(barrier, CHIPS)

    ex = [
        send(cot, cot2.at[c], ex_s.at[0], ex_r.at[0], partner),
        send(key_in, key2.at[c], ex_s.at[1], ex_r.at[1], partner),
        send(wt_in, wt2.at[c], ex_s.at[2], ex_r.at[2], partner),
    ]
    cot2[c] = cot[...]
    key2[c] = key_in[...]
    wt2[c] = wt_in[...]

    def gather_down(i, carry):
        d2 = ((dp // 4 + i // 4) % 2) * 4 + (z + i % 4) % 4
        send(down_h, down.at[dp], ag_s.at[i], ag_r.at[dp], (d2, tn))
        return carry

    lax.fori_loop(1, 8, gather_down, 0)

    o = lax.broadcasted_iota(jnp.int32, (256, 256), 0)
    i = lax.broadcasted_iota(jnp.int32, (256, 256), 1)
    perm[...] = jnp.where((o % 64) // 4 * 16 + o // 64 * 4 + o % 4 == i, 1.0, 0.0).astype(BF)
    perm_t[...] = jnp.where((i % 64) // 4 * 16 + i // 64 * 4 + i % 4 == o, 1.0, 0.0).astype(BF)

    for e in ex:
        e.wait_recv()

    def place(n, carry):
        r0 = pl.multiple_of(n * 128, 128)
        r = r0 + lax.broadcasted_iota(jnp.int32, (128, 128), 0)
        lane = lax.broadcasted_iota(jnp.int32, (128, 128), 1)
        want = jnp.where((r // 4) % 4 == lane // 32, (r // 16) * 8 + 4 * c + r % 4, -1)
        lane1 = lax.broadcasted_iota(jnp.int32, (8, 128), 1)
        first = (lane1 // 16) % 2 == 0
        keys = jnp.where(first, key2[0], key2[1])
        wts = jnp.where(first, wt2[0], wt2[1])
        one = jnp.zeros((128, 128), F32)
        wsum = jnp.zeros((128, 128), F32)
        for k in range(8):
            hit = want == keys[k : k + 1, :]
            one = jnp.where(hit, 1.0, one)
            wsum = jnp.where(hit, wts[k : k + 1, :], wsum)
        hi = wsum.astype(BF)
        lo = (wsum - hi.astype(F32)).astype(BF)
        m01[pl.ds(r0, 128), :] = one.astype(BF)
        mg[pl.ds(r0, 128), 0:128] = hi
        mg[pl.ds(r0, 128), 128:256] = lo
        one_t = jnp.transpose(one)
        w_t = jnp.transpose(wsum)
        hi_t = w_t.astype(BF)
        c01[:, pl.ds(r0, 128)] = one_t.astype(BF)
        cw[0:128, pl.ds(r0, 128)] = hi_t
        cw[128:256, pl.ds(r0, 128)] = (w_t - hi_t.astype(F32)).astype(BF)
        return carry

    lax.fori_loop(0, 8, place, 0)

    def scatter_units(src, dst, s_sem, r_sem):
        def one(i, carry):
            d2, t2 = peer(i)
            send(src.at[d2 * 8 + t2], dst.at[chip], s_sem, r_sem.at[chip // 16], (d2, t2 * 2 + c))
            return carry

        lax.fori_loop(1, CHIPS, one, 0)
        pltpu.make_async_copy(src.at[chip], dst.at[chip], r_sem.at[chip // 16]).start()

    def sent_units(src, s_sem):
        landed(src.at[pl.ds(0, CHIPS - 1)], s_sem)

    for q in range(4):
        for b in range(2):
            part = cot2[b, :, q * quarter : (q + 1) * quarter]
            row = q * 32 + b * 16
            cg[row : row + 16, :] = part
            cg[128 + row : 128 + row + 16, :] = part

    def place_cot(g, carry):
        rows = mm(mg[pl.ds(pl.multiple_of(g * 256, 256), 256), :], cg[...])
        buf_a[pl.ds(g * 16, 16)] = rows.astype(BF).reshape(16, ROWS, quarter)
        return carry

    lax.fori_loop(0, 4, place_cot, 0)
    scatter_units(buf_a, garr, ga_s, ga_r)

    load_hid.wait()

    def dense(i, carry):
        m = (dp // 2 + i) % 4
        for h in range(2):
            landed(down.at[2 * m + h], ag_r.at[2 * m + h])
            p = mm(hid[...], down[2 * m + h])
            pf[m, :, :, h * half : (h + 1) * half] = p.reshape(16, 16, half)

        def pack(t, carry):
            psend[m, t] = pf[m, 2 * t + 1 - c].astype(BF)
            return carry

        lax.fori_loop(0, 8, pack, 0)
        send(psend.at[m], prec.at[m], ps_s.at[m], ps_r.at[m], partner)
        return carry

    lax.fori_loop(0, 4, dense, 0)

    def reduce(i, carry):
        m = (dp // 2 + i) % 4
        landed(prec.at[m], ps_r.at[m])

        def add(t, carry):
            rs_send[m, t] = (pf[m, 2 * t + c] + prec[m, t].astype(F32)).astype(BF)
            return carry

        lax.fori_loop(0, 8, add, 0)

        def out(k, carry):
            t2 = ((tc // 4 + k // 4) % 2) * 4 + (y + k % 4) % 4
            send(rs_send.at[m, t2], rs_recv.at[m, tc], rs_s.at[m], rs_r.at[m], (dp, t2 * 2 + c))
            return carry

        lax.fori_loop(1, 8, out, 0)
        pltpu.make_async_copy(rs_send.at[m, tc], rs_recv.at[m, tc], rs_r.at[m]).start()
        return carry

    lax.fori_loop(0, 4, reduce, 0)

    square = jnp.zeros((16, 1), F32)
    for m in range(4):
        cols = slice(m * quarter, (m + 1) * quarter)
        landed(rs_recv.at[m], rs_r.at[m])
        total = rs_recv[m, 0].astype(F32)
        for t in range(1, 8):
            total = total + rs_recv[m, t].astype(F32)
        st = (res[:, cols].astype(F32) + total).astype(BF)
        stream[:, cols] = st
        st = st.astype(F32)
        square = square + jnp.sum(st * st, axis=1, keepdims=True)
    inverse = lax.rsqrt(square / width + 1e-6)
    nrm2[c] = (stream[...].astype(F32) * inverse * gain[...].astype(F32)).astype(BF)
    nx = send(nrm2.at[c], nrm2.at[c], ex_s.at[3], ex_r.at[3], partner)
    nx.wait_recv()

    for q in range(4):
        for b in range(2):
            row = q * 32 + b * 16
            cn[row : row + 16, :] = nrm2[b, :, q * quarter : (q + 1) * quarter]

    def place_nrm(g, carry):
        rows = mm(m01[pl.ds(pl.multiple_of(g * 256, 256), 256), :], cn[...])
        buf_b[pl.ds(g * 16, 16)] = rows.astype(BF).reshape(16, ROWS, quarter)
        return carry

    lax.fori_loop(0, 4, place_nrm, 0)
    scatter_units(buf_b, narr, na_s, na_r)

    def collect(arr, r_sem):
        def group(g, carry):
            landed(arr.at[pl.ds(g * 16, 16)], r_sem.at[g])
            rows = mm(perm[...], arr[pl.ds(g * 16, 16)].reshape(256, quarter)).astype(BF)
            for q in range(4):
                xin[pl.ds(pl.multiple_of(g * 64, 64), 64), q * quarter : (q + 1) * quarter] = rows[
                    q * 64 : (q + 1) * 64
                ]
            return carry

        lax.fori_loop(0, 4, group, 0)

    collect(garr, ga_r)
    load_wd.wait()

    def back_down(n, carry):
        at = pl.ds(pl.multiple_of(n * 256, 256), 256)
        gact[:, at] = mm_t(xin[...], wd[at, :])
        return carry

    lax.fori_loop(0, 4, back_down, 0)

    collect(narr, na_r)
    load_wg.wait()
    load_wu.wait()

    def forward(n, carry):
        at = pl.ds(pl.multiple_of(n * 256, 256), 256)
        gate = mm(xin[...], wg[:, at])
        up = mm(xin[...], wu[:, at])
        ga = gact[:, at]
        s = jax.nn.sigmoid(gate)
        silu = gate * s
        act[:, at] = (silu * up).astype(BF)
        gg[:, at] = (ga * up * s * (1.0 + gate * (1.0 - s))).astype(BF)
        gu[:, at] = (ga * silu).astype(BF)
        return carry

    lax.fori_loop(0, 4, forward, 0)

    def to_zin(q, rows):
        rows = rows.astype(BF)
        for g in range(4):
            zin[g, pl.ds(pl.multiple_of(q * 64, 64), 64), :] = rows[g * 64 : (g + 1) * 64]

    def back_in(q, carry):
        at = pl.ds(pl.multiple_of(q * quarter, 128), quarter)
        to_zin(q, mm_t(gg[...], wg[at, :]) + mm_t(gu[...], wu[at, :]))
        return carry

    def from_zin(buf):
        def group(g, carry):
            rows = mm(perm_t[...], zin[g])
            buf[pl.ds(g * 16, 16)] = rows.astype(BF).reshape(16, ROWS, quarter)
            return carry

        lax.fori_loop(0, 4, group, 0)

    lax.fori_loop(0, 4, back_in, 0)
    sent_units(buf_b, na_s)
    from_zin(buf_b)
    scatter_units(buf_b, hret, ha_s, ha_r)

    def down_out(q, carry):
        at = pl.ds(pl.multiple_of(q * quarter, 128), quarter)
        to_zin(q, mm(act[...], wd[:, at]))
        return carry

    lax.fori_loop(0, 4, down_out, 0)
    sent_units(buf_a, ga_s)
    from_zin(buf_a)
    scatter_units(buf_a, eret, ea_s, ea_r)

    def share(u):
        def pack(q, carry):
            pax[u, q] = acc[u, 2 * q + 1 - c]
            return carry

        lax.fori_loop(0, 4, pack, 0)
        return send(pax.at[u], prx.at[u], px_s.at[u], px_r.at[u], partner)

    def summed(u, q):
        return acc[u, 2 * q + c] + prx[u, q]

    total = jnp.zeros((128, quarter), F32)
    for g in range(4):
        landed(hret.at[pl.ds(g * 16, 16)], ha_r.at[g])
        total = total + mm(c01[:, g * 256 : (g + 1) * 256], hret[g * 16 : (g + 1) * 16].reshape(256, quarter))
    acc[0] = total.reshape(8, 16, quarter)
    sh0 = share(0)
    sh0.wait_recv()

    dots = jnp.zeros((16, 1), F32)
    for q in range(4):
        cols = slice(q * quarter, (q + 1) * quarter)
        scaled = summed(0, q) * gain[:, cols].astype(F32)
        dots = dots + jnp.sum(scaled * (stream[:, cols].astype(F32) * inverse), axis=1, keepdims=True)
    mean = dots / width
    for q in range(4):
        cols = slice(q * quarter, (q + 1) * quarter)
        scaled = summed(0, q) * gain[:, cols].astype(F32)
        unit = stream[:, cols].astype(F32) * inverse
        gs_o[:, cols] = (cot[:, cols].astype(F32) + inverse * (scaled - unit * mean)).astype(BF)
    gs_all[tn] = gs_o[...]

    def gather_gs(k, carry):
        t2 = ((tc // 4 + k // 4) % 2) * 4 + (y + k % 4) % 4
        send(gs_all.at[tn], gs_all.at[tn], gs_s.at[k], gs_r.at[tc], (dp, t2 * 2 + c))
        return carry

    lax.fori_loop(1, 8, gather_gs, 0)
    send(gs_all.at[tn], gs_all.at[tn], fw_s.at[tc], fw_r.at[tc], partner)

    def forward_gs(k, carry):
        t2 = ((tc // 4 + k // 4) % 2) * 4 + (y + k % 4) % 4
        b2 = t2 * 2 + c
        landed(gs_all.at[b2], gs_r.at[t2])
        send(gs_all.at[b2], gs_all.at[b2], fw_s.at[t2], fw_r.at[t2], partner)
        return carry

    lax.fori_loop(1, 8, forward_gs, 0)

    def all_gs(t, carry):
        landed(gs_all.at[t * 2 + 1 - c], fw_r.at[t])
        return carry

    lax.fori_loop(0, 8, all_gs, 0)
    rows = gs_all[...].reshape(256, width)
    gh = jnp.zeros(gh_o.shape, F32)
    for j in range(8):
        gh = gh + mm_t(rows[:, j * half : (j + 1) * half], down[j])
    gh_o[...] = gh.astype(BF)

    total = jnp.zeros((256, quarter), F32)
    for g in range(4):
        landed(eret.at[pl.ds(g * 16, 16)], ea_r.at[g])
        total = total + mm(cw[:, g * 256 : (g + 1) * 256], eret[g * 16 : (g + 1) * 16].reshape(256, quarter))
    acc[1] = (total[0:128] + total[128:256]).reshape(8, 16, quarter)
    sh1 = share(1)
    sh1.wait_recv()
    for q in range(4):
        cols = slice(q * quarter, (q + 1) * quarter)
        moe_o[:, cols] = (stream[:, cols].astype(F32) + summed(1, q)).astype(BF)

    for e in ex:
        e.wait_send()
    nx.wait_send()
    sh0.wait_send()
    sh1.wait_send()

    def down_sent(i, carry):
        landed(down_h, ag_s.at[i])
        return carry

    lax.fori_loop(1, 8, down_sent, 0)

    def rest_sent(m, carry):
        landed(psend.at[m], ps_s.at[m])
        landed(rs_send.at[m, pl.ds(0, 7)], rs_s.at[m])
        return carry

    lax.fori_loop(0, 4, rest_sent, 0)
    sent_units(buf_b, ha_s)
    sent_units(buf_a, ea_s)

    def gs_sent(k, carry):
        landed(gs_all.at[0], gs_s.at[k])
        return carry

    lax.fori_loop(1, 8, gs_sent, 0)

    def fw_sent(k, carry):
        landed(gs_all.at[0], fw_s.at[k])
        return carry

    lax.fori_loop(0, 8, fw_sent, 0)


def body(
    dense_hidden, dense_down, residual, norm_gain, expert_ids, route_weights,
    w_gate, w_up, w_down, out_cotangent,
):
    width = residual.shape[1]
    q = width // 4
    hidden_units, cols = dense_down.shape
    fe = w_gate.shape[2]
    core = lax.axis_index("tensor") % 2
    flat = expert_ids.reshape(-1)
    order = jnp.arange(flat.shape[0], dtype=jnp.int32)
    same = (flat[:, None] == flat[None, :]) & (order[None, :] < order[:, None])
    slot = jnp.sum(same.astype(jnp.int32), axis=1).reshape(expert_ids.shape)
    key = jnp.tile((expert_ids * 4 + slot + 2 * core).T, (1, 8))
    wt = jnp.tile(route_weights.T, (1, 8))

    vmem = pl.BlockSpec(memory_space=pltpu.VMEM)
    hbm = pl.BlockSpec(memory_space=pl.ANY)
    V = pltpu.VMEM
    dma = pltpu.SemaphoreType.DMA
    unit = (CHIPS, ROWS, q)
    scratch = [
        V((256, hidden_units), BF), V((8, hidden_units, cols), BF),
        V((width, fe), BF), V((width, fe), BF), V((fe, width), BF),
        V((2, 16, width), BF), V((2, 8, 128), jnp.int32), V((2, 8, 128), F32), V((2, 16, width), BF),
        V((1024, 128), BF), V((1024, 256), BF), V((128, 1024), BF), V((256, 1024), BF),
        V((256, 256), BF), V((256, 256), BF), V((128, q), BF), V((256, q), BF),
        V(unit, BF), V(unit, BF), V(unit, BF), V(unit, BF), V(unit, BF), V(unit, BF),
        V((256, width), BF), V((256, fe), F32), V((256, fe), BF), V((256, fe), BF), V((256, fe), BF),
        V((4, 256, q), BF),
        V((4, 16, 16, q), F32), V((4, 8, 16, q), BF), V((4, 8, 16, q), BF), V((4, 8, 16, q), BF),
        V((4, 8, 16, q), BF), V((16, width), BF),
        V((2, 8, 16, q), F32), V((2, 4, 16, q), F32), V((2, 4, 16, q), F32), V((16, 16, width), BF),
        dma((4,)), dma((4,)), dma((4,)), dma((8,)), dma((8,)), dma((4,)), dma((4,)), dma((4,)), dma((4,)),
        dma, dma((4,)), dma, dma((4,)), dma, dma((4,)), dma, dma((4,)),
        dma((2,)), dma((2,)), dma((8,)), dma((8,)), dma((8,)), dma((8,)),
    ]
    return pl.pallas_call(
        kernel,
        out_shape=(
            jax.ShapeDtypeStruct(residual.shape, BF),
            jax.ShapeDtypeStruct(residual.shape, BF),
            jax.ShapeDtypeStruct(dense_hidden.shape, BF),
        ),
        in_specs=[hbm, hbm, vmem, vmem, vmem, vmem, vmem, hbm, hbm, hbm],
        out_specs=(vmem, vmem, vmem),
        scratch_shapes=scratch,
        compiler_params=pltpu.CompilerParams(
            collective_id=0, has_side_effects=True, vmem_limit_bytes=63 * 1024 * 1024
        ),
    )(
        dense_hidden, dense_down, residual, norm_gain.reshape(1, width), out_cotangent, key, wt,
        w_gate[0], w_up[0], w_down[0],
    )


def solution(mesh):
    rows = P(("dp", "tensor"), None)
    experts = P(("dp", "tensor"), None, None)
    placed = (P("dp", "tensor"), P("tensor", "dp"), rows, P(), rows, rows, experts, experts, experts, rows)
    return jax.shard_map(
        body, mesh=mesh, in_specs=placed, out_specs=(rows, rows, P("dp", "tensor")), check_vma=False
    )
```

time: 416 us -> 229 us (0.55)
  Pallas kernels: 0 us -> 212 us
  waiting for transfers between devices: 195 us -> 0 us
  blocking collectives: 102 us -> 0 us
  local copies, waits for them, and re-layouts: 56.1 us -> 13.2 us
  matrix products: 30.4 us -> 0 us
  between operations: 14.4 us -> 0.67 us
  starting transfers between devices: 6.63 us -> 0 us
  other arithmetic: 4.59 us -> 0.19 us
    pallas_call x0 -> x1, Pallas kernels: none -> 212 us  [body(): pl.pallas_call(kernel, out_shape=(jax.ShapeDtypeStruct(residual.shape, BF...]
    all_gather x2 -> x0, waiting for transfers between devices: 108 us -> none  [the longest x1 77.5 us: body(): down_full = lax.all_gather(dense_down, 'dp', axis=1, tiled=True)]
    all_to_all x3 -> x0, blocking collectives: 102 us -> none  [the longest x2 70 us: to_experts(): lax.all_to_all(rows, ('dp', 'tensor'), split_axis=1, concat_axis=1, tiled...]
    reduce_scatter x1 -> x0, waiting for transfers between devices: 60.5 us -> none  [body(): lax.psum_scatter(jnp.dot(dense_hidden, down_full, preferred_element_type=...]
    scatter x4 -> x0, local copies, waits for them, and re-layouts: 39.2 us -> none  [the longest x2 19.6 us: body(): send = jnp.zeros((capacity, devices, model_width), jnp.bfloat16).at[slot_...]
    dot_general x8 -> x0, matrix products: 30.4 us -> none  [the longest x1 5.77 us: body(): jnp.dot(dense_hidden, down_full, preferred_element_type=jnp.float32)]
    all_to_all x1 -> x0, waiting for transfers between devices: 26.3 us -> none  [to_tokens(): lax.all_to_all(rows, ('dp', 'tensor'), split_axis=1, concat_axis=1, tiled...]
    gather x2 -> x0, local copies, waits for them, and re-layouts: 7.11 us -> none  [the longest x1 3.55 us: body(): picked = returned[slot_index, expert_ids].astype(jnp.float32)]
  transfers between devices with their start and end apart: 4 -> 0, of which waited for: 4 -> 0; matrix products, arithmetic and copies ran while one was open for 0% -> 0% of each run, Pallas kernels for 0% -> 0%
where the time goes in v1:
time: 229 us; the launch traced here: 226 us
  Pallas kernels  212 us (93%)
  local copies, waits for them, and re-layouts  13.2 us (6%)
    pallas_call x1, Pallas kernels, body(): pl.pallas_call(kernel, out_shape=(jax.ShapeDtypeStruct(residual.shape, BF...  212 us
    unnamed x5, local copies, waits for them, and re-layouts  7.81 us

profile of v1, /device:TPU:33, one launch (start us, length us, event | category | flops | bytes accessed | tf_op | source)
XLA Modules:
  0.0 225.6 jit_solution(12137071608433188656)
XLA Ops:
  0.6 0.8 copy.25
  1.4 0.1 eq.17
  1.5 0.2 convert_reduce_fusion
  1.7 0.1 reshape.23
  1.8 0.1 copy.27
  1.8 1.3 reshape.22.gain
  3.2 0.7 tile.9.key_in
  3.8 0.7 tile.20
  4.5 0.7 tile.21.wt_in
  5.2 1.9 copy.28.hid_h
  7.1 2.1 copy.29.down_h
  9.1 211.5 %shard_map.121 = (bf16[16,3584]{1,0:T(8,128)(2,1)}, bf16[16,3584]{1,0:T(8,128)(2,1)}, bf16[256,576]{1,0:T(8,128)(2,1)}) custom-call(bf16[256,576]{1,0:T(8,128)(2,1)} %copy.28.hid_h, bf16[576,448]{1,0:T(8,128)(2,1)} %copy.29.down_h, bf16[16,3584]{1,0:T(8,128)(2,1)} %res.1, bf16[1,3584]{1,0:T(2,128)(2,1)} %reshape.22.gain, bf16[16,3584]{1,0:T(8,128)(2,1)} %cot.1, ...), custom_call_target="tpu_custom_call" | custom-call | tf_op jit(solution)/shard_map/pallas_call | solution.py:453
  220.7 1.8 copy.30
  222.5 1.6 copy.33
  224.1 1.6 copy.34
  (2 shorter events, 0.0 us)

commit v2 on v1

--- a/solution.py
+++ b/solution.py
@@ -9,6 +9,7 @@
 BF = jnp.bfloat16
 F32 = jnp.float32
 CHIPS = 64
+EARLY = 24
 ROWS = 16
 NT = (((1,), (1,)), ((), ()))
 
@@ -26,16 +27,16 @@
 
 
 def kernel(
-    hid_h, down_h, res, gain, cot, key_in, wt_in, wg_h, wu_h, wd_h,
+    hid_h, down_h, res, gain_in, cot, ids_in, wt_in, wg_h, wu_h, wd_h,
     moe_o, gs_o, gh_o,
-    hid, down, wg, wu, wd,
-    cot2, key2, wt2, nrm2,
+    hid, down_t, down2, wg, wu, wd,
+    gain, cot2, key2, wt2, nrm2,
     m01, mg, c01, cw, perm, perm_t, cn, cg,
     buf_a, garr, buf_b, narr, hret, eret,
     xin, gact, act, gg, gu, zin,
-    pf, psend, prec, rs_send, rs_recv, stream,
-    acc, pax, prx, gs_all,
-    loc, ex_s, ex_r, ag_s, ag_r, ps_s, ps_r, rs_s, rs_r,
+    pf, psend, prec, rs_send, rs_recv, zxs, zxr, dense_f, stream,
+    acc, pax, prx, gsp, gs_all, ghs, ghr,
+    loc, ex_s, ex_r, hg_s, hg_r, dg_s, dg_r, zx_s, zx_r, gx_s, gx_r, gh_s, gh_r, ps_s, ps_r, rs_s, rs_r,
     ga_s, ga_r, na_s, na_r, ha_s, ha_r, ea_s, ea_r, px_s, px_r, gs_s, gs_r, fw_s, fw_r,
 ):
     width = res.shape[1]
@@ -47,13 +48,16 @@
     tc = tn // 2
     chip = dp * 8 + tc
     z, y = dp % 4, tc % 4
-    x = (dp // 4) * 2 + tc // 4
+    xh = dp // 4
+    x = xh * 2 + tc // 4
+    over_x = ((1 - xh) * 4 + z, tn)
     partner = (dp, tc * 2 + 1 - c)
 
     def peer(i):
-        x2 = (x + i % 4) % 4
-        y2 = (y + (i // 4) % 4) % 4
-        z2 = (z + i // 16) % 4
+        u = i // 4 % 4
+        x2 = (x + i) % 4
+        y2 = (y + i + u) % 4
+        z2 = (z + i + 2 * u + i // 16) % 4
         return (x2 // 2) * 4 + z2, (x2 % 2) * 4 + y2
 
     def send(src, dst, s_sem, r_sem, device):
@@ -64,9 +68,17 @@
         copy.start()
         return copy
 
-    pltpu.make_async_copy(down_h, down.at[dp], ag_r.at[dp]).start()
-    load_hid = pltpu.make_async_copy(hid_h, hid, loc.at[0])
-    load_hid.start()
+    pending = []
+
+    def drain():
+        for done in pending:
+            done()
+
+    def block(h):
+        return down_t.at[pl.ds(pl.multiple_of(h * half, 16), half)]
+
+    pltpu.make_async_copy(down_h, block(xh), dg_r.at[xh]).start()
+    pltpu.make_async_copy(hid_h, hid.at[z], hg_r.at[z]).start()
     load_wd = pltpu.make_async_copy(wd_h, wd, loc.at[1])
     load_wg = pltpu.make_async_copy(wg_h, wg, loc.at[2])
     load_wu = pltpu.make_async_copy(wu_h, wu, loc.at[3])
@@ -83,47 +95,60 @@
 
     lax.fori_loop(1, CHIPS, greet, 0)
     pl.semaphore_signal(barrier, inc=1, device_id=partner, device_id_type=MESH)
+
+    lane = lax.broadcasted_iota(jnp.int32, (16, 128), 1)
+    spread = jnp.where(lane % 16 == lax.broadcasted_iota(jnp.int32, (16, 128), 0), 1.0, 0.0)
+
+    def lanes(a):
+        return jnp.dot(a, spread, precision=lax.Precision.HIGHEST, preferred_element_type=F32)
+
+    key2[c] = lanes(ids_in[...].astype(F32))
+    wt2[c] = lanes(wt_in[...])
+    cot2[c] = cot[...]
+    gain[...] = gain_in[...].reshape(1, width)
     pl.semaphore_wait(barrier, CHIPS)
 
     ex = [
-        send(cot, cot2.at[c], ex_s.at[0], ex_r.at[0], partner),
-        send(key_in, key2.at[c], ex_s.at[1], ex_r.at[1], partner),
-        send(wt_in, wt2.at[c], ex_s.at[2], ex_r.at[2], partner),
+        send(key2.at[c], key2.at[c], ex_s.at[1], ex_r.at[1], partner),
+        send(wt2.at[c], wt2.at[c], ex_s.at[2], ex_r.at[2], partner),
+        send(cot2.at[c], cot2.at[c], ex_s.at[0], ex_r.at[0], partner),
     ]
-    cot2[c] = cot[...]
-    key2[c] = key_in[...]
-    wt2[c] = wt_in[...]
-
-    def gather_down(i, carry):
-        d2 = ((dp // 4 + i // 4) % 2) * 4 + (z + i % 4) % 4
-        send(down_h, down.at[dp], ag_s.at[i], ag_r.at[dp], (d2, tn))
-        return carry
-
-    lax.fori_loop(1, 8, gather_down, 0)
+
+    over_z = [(xh * 4 + (z + k) % 4, tn) for k in range(4)]
+    for k in (2, 1, 3):
+        pending.append(send(hid_h, hid.at[z], hg_s.at[k], hg_r.at[z], over_z[k]).wait_send)
+    pending.append(send(down_h, block(xh), dg_s, dg_r.at[xh], over_x).wait_send)
 
     o = lax.broadcasted_iota(jnp.int32, (256, 256), 0)
     i = lax.broadcasted_iota(jnp.int32, (256, 256), 1)
     perm[...] = jnp.where((o % 64) // 4 * 16 + o // 64 * 4 + o % 4 == i, 1.0, 0.0).astype(BF)
     perm_t[...] = jnp.where((i % 64) // 4 * 16 + i // 64 * 4 + i % 4 == o, 1.0, 0.0).astype(BF)
 
+    pending.extend(e.wait_send for e in ex)
     for e in ex:
         e.wait_recv()
 
+    row = lax.broadcasted_iota(jnp.int32, (128, 128), 0)
+    lane = lax.broadcasted_iota(jnp.int32, (128, 128), 1)
+    earlier = jnp.where((row // 16 == lane // 16) & (row < lane), 1.0, 0.0).astype(BF)
+    first = (lax.broadcasted_iota(jnp.int32, (8, 128), 1) // 16) % 2 == 0
+    keys = jnp.where(first, key2[0], key2[1])
+    wts = jnp.where(first, wt2[0], wt2[1])
+
     def place(n, carry):
         r0 = pl.multiple_of(n * 128, 128)
-        r = r0 + lax.broadcasted_iota(jnp.int32, (128, 128), 0)
-        lane = lax.broadcasted_iota(jnp.int32, (128, 128), 1)
-        want = jnp.where((r // 4) % 4 == lane // 32, (r // 16) * 8 + 4 * c + r % 4, -1)
-        lane1 = lax.broadcasted_iota(jnp.int32, (8, 128), 1)
-        first = (lane1 // 16) % 2 == 0
-        keys = jnp.where(first, key2[0], key2[1])
-        wts = jnp.where(first, wt2[0], wt2[1])
-        one = jnp.zeros((128, 128), F32)
-        wsum = jnp.zeros((128, 128), F32)
+        r = r0 + row
+        expert = ((r // 16) * 2 + c).astype(F32)
+        member = jnp.zeros((128, 128), F32)
+        weight = jnp.zeros((128, 128), F32)
         for k in range(8):
-            hit = want == keys[k : k + 1, :]
-            one = jnp.where(hit, 1.0, one)
-            wsum = jnp.where(hit, wts[k : k + 1, :], wsum)
+            hit = jnp.abs(keys[k : k + 1, :] - expert) < 0.5
+            member = jnp.where(hit, 1.0, member)
+            weight = jnp.where(hit, wts[k : k + 1, :], weight)
+        slot = mm(member.astype(BF), earlier) + (lane // 16 % 2 * 2).astype(F32)
+        here = ((r // 4) % 4 == lane // 32) & (jnp.abs(slot - (r % 4).astype(F32)) < 0.5)
+        one = jnp.where(here, member, 0.0)
+        wsum = jnp.where(here, weight, 0.0)
         hi = wsum.astype(BF)
         lo = (wsum - hi.astype(F32)).astype(BF)
         m01[pl.ds(r0, 128), :] = one.astype(BF)
@@ -139,14 +164,15 @@
 
     lax.fori_loop(0, 8, place, 0)
 
-    def scatter_units(src, dst, s_sem, r_sem):
+    def scatter_units(src, dst, s_sem, r_sem, lo=1, hi=CHIPS):
         def one(i, carry):
             d2, t2 = peer(i)
             send(src.at[d2 * 8 + t2], dst.at[chip], s_sem, r_sem.at[chip // 16], (d2, t2 * 2 + c))
             return carry
 
-        lax.fori_loop(1, CHIPS, one, 0)
-        pltpu.make_async_copy(src.at[chip], dst.at[chip], r_sem.at[chip // 16]).start()
+        lax.fori_loop(lo, hi, one, 0)
+        if hi == CHIPS:
+            pltpu.make_async_copy(src.at[chip], dst.at[chip], r_sem.at[chip // 16]).start()
 
     def sent_units(src, s_sem):
         landed(src.at[pl.ds(0, CHIPS - 1)], s_sem)
@@ -164,16 +190,18 @@
         return carry
 
     lax.fori_loop(0, 4, place_cot, 0)
-    scatter_units(buf_a, garr, ga_s, ga_r)
-
-    load_hid.wait()
+    scatter_units(buf_a, garr, ga_s, ga_r, 1, EARLY)
+
+    for h in range(2):
+        landed(block(h), dg_r.at[h])
+
+    def turn(i):
+        return (z + i + i // 2 - i // 3 * 2) % 4
 
     def dense(i, carry):
-        m = (dp // 2 + i) % 4
-        for h in range(2):
-            landed(down.at[2 * m + h], ag_r.at[2 * m + h])
-            p = mm(hid[...], down[2 * m + h])
-            pf[m, :, :, h * half : (h + 1) * half] = p.reshape(16, 16, half)
+        m = turn(i)
+        landed(hid.at[m], hg_r.at[m])
+        pf[m] = mm_t(jnp.transpose(hid[m]), down_t[...]).reshape(16, 16, quarter)
 
         def pack(t, carry):
             psend[m, t] = pf[m, 2 * t + 1 - c].astype(BF)
@@ -186,7 +214,7 @@
     lax.fori_loop(0, 4, dense, 0)
 
     def reduce(i, carry):
-        m = (dp // 2 + i) % 4
+        m = turn(i)
         landed(prec.at[m], ps_r.at[m])
 
         def add(t, carry):
@@ -206,21 +234,53 @@
 
     lax.fori_loop(0, 4, reduce, 0)
 
-    square = jnp.zeros((16, 1), F32)
-    for m in range(4):
-        cols = slice(m * quarter, (m + 1) * quarter)
+    def sums_sent():
+        def one(m, carry):
+            landed(psend.at[m], ps_s.at[m])
+            landed(rs_send.at[m, pl.ds(0, 7)], rs_s.at[m])
+            return carry
+
+        lax.fori_loop(0, 4, one, 0)
+
+    pending.append(sums_sent)
+
+    def to_owner(i, carry):
+        m = turn(i)
         landed(rs_recv.at[m], rs_r.at[m])
         total = rs_recv[m, 0].astype(F32)
         for t in range(1, 8):
             total = total + rs_recv[m, t].astype(F32)
-        st = (res[:, cols].astype(F32) + total).astype(BF)
-        stream[:, cols] = st
-        st = st.astype(F32)
-        square = square + jnp.sum(st * st, axis=1, keepdims=True)
+        zxs[m] = total
+
+        @pl.when(i > 0)
+        def _():
+            send(zxs.at[m], zxr.at[z], zx_s.at[m], zx_r.at[z], (xh * 4 + m, tn))
+
+        return carry
+
+    lax.fori_loop(0, 4, to_owner, 0)
+    scatter_units(buf_a, garr, ga_s, ga_r, EARLY, CHIPS)
+    pltpu.make_async_copy(zxs.at[z], zxr.at[z], zx_r.at[z]).start()
+
+    def owner_sent():
+        for k in range(1, 4):
+            landed(zxs.at[0], zx_s.at[(z + k) % 4])
+
+    pending.append(owner_sent)
+    for m in range(4):
+        landed(zxr.at[m], zx_r.at[m])
+        for h in range(2):
+            at = (4 * h + m) * half
+            dense_f[:, at : at + half] = zxr[m, :, h * half : (h + 1) * half]
+    st = (res[...].astype(F32) + dense_f[...]).astype(BF)
+    stream[...] = st
+    st = st.astype(F32)
+    square = jnp.sum(st * st, axis=1, keepdims=True)
     inverse = lax.rsqrt(square / width + 1e-6)
     nrm2[c] = (stream[...].astype(F32) * inverse * gain[...].astype(F32)).astype(BF)
     nx = send(nrm2.at[c], nrm2.at[c], ex_s.at[3], ex_r.at[3], partner)
     nx.wait_recv()
+    pending.append(nx.wait_send)
 
     for q in range(4):
         for b in range(2):
@@ -234,6 +294,8 @@
 
     lax.fori_loop(0, 4, place_nrm, 0)
     scatter_units(buf_b, narr, na_s, na_r)
+
+    down2[...] = jnp.transpose(down_t[...])
 
     def collect(arr, r_sem):
         def group(g, carry):
@@ -297,6 +359,7 @@
     sent_units(buf_b, na_s)
     from_zin(buf_b)
     scatter_units(buf_b, hret, ha_s, ha_r)
+    pending.append(lambda: sent_units(buf_b, ha_s))
 
     def down_out(q, carry):
         at = pl.ds(pl.multiple_of(q * quarter, 128), quarter)
@@ -307,6 +370,7 @@
     sent_units(buf_a, ga_s)
     from_zin(buf_a)
     scatter_units(buf_a, eret, ea_s, ea_r)
+    pending.append(lambda: sent_units(buf_a, ea_s))
 
     def share(u):
         def pack(q, carry):
@@ -326,6 +390,7 @@
     acc[0] = total.reshape(8, 16, quarter)
     sh0 = share(0)
     sh0.wait_recv()
+    pending.append(sh0.wait_send)
 
     dots = jnp.zeros((16, 1), F32)
     for q in range(4):
@@ -338,7 +403,17 @@
         scaled = summed(0, q) * gain[:, cols].astype(F32)
         unit = stream[:, cols].astype(F32) * inverse
         gs_o[:, cols] = (cot[:, cols].astype(F32) + inverse * (scaled - unit * mean)).astype(BF)
-    gs_all[tn] = gs_o[...]
+
+    for m in range(4):
+        for h in range(2):
+            at = (4 * h + m) * half
+            gsp[m, :, h * half : (h + 1) * half] = gs_o[:, at : at + half]
+    for k in (2, 1, 3):
+        to = (z + k) % 4
+        pending.append(send(gsp.at[to], gs_all.at[tn, z], gx_s.at[k], gx_r.at[z], over_z[k]).wait_send)
+    pltpu.make_async_copy(gsp.at[z], gs_all.at[tn, z], gx_r.at[z]).start()
+    for m in range(4):
+        landed(gs_all.at[tn, m], gx_r.at[m])
 
     def gather_gs(k, carry):
         t2 = ((tc // 4 + k // 4) % 2) * 4 + (y + k % 4) % 4
@@ -357,16 +432,32 @@
 
     lax.fori_loop(1, 8, forward_gs, 0)
 
+    def gs_sent():
+        def one(k, carry):
+            landed(gs_all.at[0], gs_s.at[k])
+            return carry
+
+        lax.fori_loop(1, 8, one, 0)
+
+        def two(k, carry):
+            landed(gs_all.at[0], fw_s.at[k])
+            return carry
+
+        lax.fori_loop(0, 8, two, 0)
+
+    pending.append(gs_sent)
+
     def all_gs(t, carry):
         landed(gs_all.at[t * 2 + 1 - c], fw_r.at[t])
         return carry
 
     lax.fori_loop(0, 8, all_gs, 0)
-    rows = gs_all[...].reshape(256, width)
-    gh = jnp.zeros(gh_o.shape, F32)
-    for j in range(8):
-        gh = gh + mm_t(rows[:, j * half : (j + 1) * half], down[j])
-    gh_o[...] = gh.astype(BF)
+    for k in (2, 1, 3, 0):
+        to = (z + k) % 4
+        gh = mm_t(down2[...], gs_all[:, to].reshape(256, quarter))
+        ghs[k] = gh.astype(BF)
+        if k:
+            pending.append(send(ghs.at[k], ghr.at[z], gh_s.at[k], gh_r.at[z], over_z[k]).wait_send)
 
     total = jnp.zeros((256, quarter), F32)
     for g in range(4):
@@ -375,42 +466,24 @@
     acc[1] = (total[0:128] + total[128:256]).reshape(8, 16, quarter)
     sh1 = share(1)
     sh1.wait_recv()
+    pending.append(sh1.wait_send)
     for q in range(4):
         cols = slice(q * quarter, (q + 1) * quarter)
         moe_o[:, cols] = (stream[:, cols].astype(F32) + summed(1, q)).astype(BF)
 
-    for e in ex:
-        e.wait_send()
-    nx.wait_send()
-    sh0.wait_send()
-    sh1.wait_send()
-
-    def down_sent(i, carry):
-        landed(down_h, ag_s.at[i])
-        return carry
-
-    lax.fori_loop(1, 8, down_sent, 0)
-
-    def rest_sent(m, carry):
-        landed(psend.at[m], ps_s.at[m])
-        landed(rs_send.at[m, pl.ds(0, 7)], rs_s.at[m])
-        return carry
-
-    lax.fori_loop(0, 4, rest_sent, 0)
-    sent_units(buf_b, ha_s)
-    sent_units(buf_a, ea_s)
-
-    def gs_sent(k, carry):
-        landed(gs_all.at[0], gs_s.at[k])
-        return carry
-
-    lax.fori_loop(1, 8, gs_sent, 0)
-
-    def fw_sent(k, carry):
-        landed(gs_all.at[0], fw_s.at[k])
-        return carry
-
-    lax.fori_loop(0, 8, fw_sent, 0)
+    for k in (1, 3, 2):
+        at = (z + k) % 4
+        landed(ghr.at[at], gh_r.at[at])
+        gh = gh + ghr[at].astype(F32)
+    gh_o[...] = gh.astype(BF)
+
+    drain()
+
+
+def hand_over(a, b, c, a_o, b_o, c_o):
+    a_o[...] = a[...]
+    b_o[...] = b[...]
+    c_o[...] = c[...]
 
 
 def body(
@@ -421,13 +494,6 @@
     q = width // 4
     hidden_units, cols = dense_down.shape
     fe = w_gate.shape[2]
-    core = lax.axis_index("tensor") % 2
-    flat = expert_ids.reshape(-1)
-    order = jnp.arange(flat.shape[0], dtype=jnp.int32)
-    same = (flat[:, None] == flat[None, :]) & (order[None, :] < order[:, None])
-    slot = jnp.sum(same.astype(jnp.int32), axis=1).reshape(expert_ids.shape)
-    key = jnp.tile((expert_ids * 4 + slot + 2 * core).T, (1, 8))
-    wt = jnp.tile(route_weights.T, (1, 8))
 
     vmem = pl.BlockSpec(memory_space=pltpu.VMEM)
     hbm = pl.BlockSpec(memory_space=pl.ANY)
@@ -435,27 +501,28 @@
     dma = pltpu.SemaphoreType.DMA
     unit = (CHIPS, ROWS, q)
     scratch = [
-        V((256, hidden_units), BF), V((8, hidden_units, cols), BF),
+        V((4, hidden_units, 256), BF), V((2 * cols, hidden_units), BF), V((hidden_units, q), BF),
         V((width, fe), BF), V((width, fe), BF), V((fe, width), BF),
-        V((2, 16, width), BF), V((2, 8, 128), jnp.int32), V((2, 8, 128), F32), V((2, 16, width), BF),
+        V((1, width), BF), V((2, 16, width), BF), V((2, 8, 128), F32), V((2, 8, 128), F32), V((2, 16, width), BF),
         V((1024, 128), BF), V((1024, 256), BF), V((128, 1024), BF), V((256, 1024), BF),
         V((256, 256), BF), V((256, 256), BF), V((128, q), BF), V((256, q), BF),
         V(unit, BF), V(unit, BF), V(unit, BF), V(unit, BF), V(unit, BF), V(unit, BF),
         V((256, width), BF), V((256, fe), F32), V((256, fe), BF), V((256, fe), BF), V((256, fe), BF),
         V((4, 256, q), BF),
         V((4, 16, 16, q), F32), V((4, 8, 16, q), BF), V((4, 8, 16, q), BF), V((4, 8, 16, q), BF),
-        V((4, 8, 16, q), BF), V((16, width), BF),
-        V((2, 8, 16, q), F32), V((2, 4, 16, q), F32), V((2, 4, 16, q), F32), V((16, 16, width), BF),
-        dma((4,)), dma((4,)), dma((4,)), dma((8,)), dma((8,)), dma((4,)), dma((4,)), dma((4,)), dma((4,)),
+        V((4, 8, 16, q), BF), V((4, 16, q), F32), V((4, 16, q), F32), V((16, width), F32), V((16, width), BF),
+        V((2, 8, 16, q), F32), V((2, 4, 16, q), F32), V((2, 4, 16, q), F32), V((4, 16, q), BF), V((16, 4, 16, q), BF),
+        V((4, hidden_units, 256), BF), V((4, hidden_units, 256), BF),
+        dma((4,)), dma((4,)), dma((4,)), dma((4,)), dma((4,)), dma, dma((2,)), dma((4,)), dma((4,)), dma((4,)), dma((4,)), dma((4,)), dma((4,)), dma((4,)), dma((4,)), dma((4,)), dma((4,)),
         dma, dma((4,)), dma, dma((4,)), dma, dma((4,)), dma, dma((4,)),
         dma((2,)), dma((2,)), dma((8,)), dma((8,)), dma((8,)), dma((8,)),
     ]
-    return pl.pallas_call(
+    moe, gs, gh = pl.pallas_call(
         kernel,
         out_shape=(
             jax.ShapeDtypeStruct(residual.shape, BF),
             jax.ShapeDtypeStruct(residual.shape, BF),
-            jax.ShapeDtypeStruct(dense_hidden.shape, BF),
+            jax.ShapeDtypeStruct(dense_hidden.shape[::-1], BF),
         ),
         in_specs=[hbm, hbm, vmem, vmem, vmem, vmem, vmem, hbm, hbm, hbm],
         out_specs=(vmem, vmem, vmem),
@@ -464,9 +531,16 @@
             collective_id=0, has_side_effects=True, vmem_limit_bytes=63 * 1024 * 1024
         ),
     )(
-        dense_hidden, dense_down, residual, norm_gain.reshape(1, width), out_cotangent, key, wt,
+        dense_hidden.T, dense_down.T, residual, norm_gain, out_cotangent, expert_ids.T, route_weights.T,
         w_gate[0], w_up[0], w_down[0],
     )
+    moe, gs, gh = pl.pallas_call(
+        hand_over,
+        out_shape=tuple(jax.ShapeDtypeStruct(a.shape, a.dtype) for a in (moe, gs, gh)),
+        in_specs=[vmem] * 3,
+        out_specs=(vmem,) * 3,
+    )(moe, gs, gh)
+    return moe, gs, gh.T
 
 
 def solution(mesh):

time: 229 us -> 184 us (0.80)
  the two profiles are of different devices: /device:TPU:33 before, /device:TPU:5 now
where the time goes in v2:
time: 184 us
  Pallas kernels  183 us (99%)
    pallas_call x1, Pallas kernels, body(): pl.pallas_call(kernel, out_shape=(jax.ShapeDtypeStruct(residual.shape, BF...  181 us

profile of v2, /device:TPU:5, one launch (start us, length us, event | category | flops | bytes accessed | tf_op | source)
XLA Modules:
  0.0 183.8 jit_solution(2039602527715100848)
XLA Ops:
  0.6 181.3 %shard_map.121 = (bf16[16,3584]{1,0:T(8,128)(2,1)}, bf16[16,3584]{1,0:T(8,128)(2,1)}, bf16[576,256]{1,0:T(8,128)(2,1)}) custom-call(bf16[576,256]{1,0:T(8,128)(2,1)} %bitcast.12, bf16[448,576]{1,0:T(8,128)(2,1)} %bitcast.11, bf16[16,3584]{1,0:T(8,128)(2,1)} %res.1, bf16[3584]{0:T(1024)(128)(2,1)} %gain_in.1, bf16[16,3584]{1,0:T(8,128)(2,1)} %cot.1, ...), custom_call_target="tpu_custom_call" | custom-call | tf_op jit(solution)/shard_map/pallas_call | solution.py:520
  182.0 1.9 %shard_map.122 = (bf16[16,3584]{1,0:T(8,128)(2,1)}, bf16[16,3584]{1,0:T(8,128)(2,1)}, bf16[576,256]{1,0:T(8,128)(2,1)}) custom-call(bf16[16,3584]{1,0:T(8,128)(2,1)} %get-tuple-element.9.a, bf16[16,3584]{1,0:T(8,128)(2,1)} %get-tuple-element.10.b, bf16[576,256]{1,0:T(8,128)(2,1)} %get-tuple-element.11.c), custom_call_target="tpu_custom_call" | custom-call | tf_op jit(solution)/shard_map/pallas_call | solution.py:537

commit v3 on v2

--- a/solution.py
+++ b/solution.py
@@ -9,7 +9,8 @@
 BF = jnp.bfloat16
 F32 = jnp.float32
 CHIPS = 64
-EARLY = 24
+COT = (6, 16)
+OUT = (22, 14, 10, 2)
 ROWS = 16
 NT = (((1,), (1,)), ((), ()))
 
@@ -33,7 +34,7 @@
     gain, cot2, key2, wt2, nrm2,
     m01, mg, c01, cw, perm, perm_t, cn, cg,
     buf_a, garr, buf_b, narr, hret, eret,
-    xin, gact, act, gg, gu, zin,
+    xin, gates, ups, act, gg, gu, zin,
     pf, psend, prec, rs_send, rs_recv, zxs, zxr, dense_f, stream,
     acc, pax, prx, gsp, gs_all, ghs, ghr,
     loc, ex_s, ex_r, hg_s, hg_r, dg_s, dg_r, zx_s, zx_r, gx_s, gx_r, gh_s, gh_r, ps_s, ps_r, rs_s, rs_r,
@@ -82,9 +83,6 @@
     load_wd = pltpu.make_async_copy(wd_h, wd, loc.at[1])
     load_wg = pltpu.make_async_copy(wg_h, wg, loc.at[2])
     load_wu = pltpu.make_async_copy(wu_h, wu, loc.at[3])
-    load_wd.start()
-    load_wg.start()
-    load_wu.start()
 
     barrier = pltpu.get_barrier_semaphore()
 
@@ -115,9 +113,13 @@
     ]
 
     over_z = [(xh * 4 + (z + k) % 4, tn) for k in range(4)]
-    for k in (2, 1, 3):
+    pending.append(send(down_h, block(xh), dg_s, dg_r.at[xh], over_x).wait_send)
+    for k in (1, 3, 2):
         pending.append(send(hid_h, hid.at[z], hg_s.at[k], hg_r.at[z], over_z[k]).wait_send)
-    pending.append(send(down_h, block(xh), dg_s, dg_r.at[xh], over_x).wait_send)
+
+    load_wg.start()
+    load_wu.start()
+    load_wd.start()
 
     o = lax.broadcasted_iota(jnp.int32, (256, 256), 0)
     i = lax.broadcasted_iota(jnp.int32, (256, 256), 1)
@@ -164,15 +166,17 @@
 
     lax.fori_loop(0, 8, place, 0)
 
-    def scatter_units(src, dst, s_sem, r_sem, lo=1, hi=CHIPS):
+    def some_units(src, dst, s_sem, r_sem, lo, count):
         def one(i, carry):
-            d2, t2 = peer(i)
+            d2, t2 = peer(lo + i)
             send(src.at[d2 * 8 + t2], dst.at[chip], s_sem, r_sem.at[chip // 16], (d2, t2 * 2 + c))
             return carry
 
-        lax.fori_loop(lo, hi, one, 0)
-        if hi == CHIPS:
-            pltpu.make_async_copy(src.at[chip], dst.at[chip], r_sem.at[chip // 16]).start()
+        lax.fori_loop(0, count, one, 0)
+
+    def scatter_units(src, dst, s_sem, r_sem, lo=1):
+        some_units(src, dst, s_sem, r_sem, lo, CHIPS - lo)
+        pltpu.make_async_copy(src.at[chip], dst.at[chip], r_sem.at[chip // 16]).start()
 
     def sent_units(src, s_sem):
         landed(src.at[pl.ds(0, CHIPS - 1)], s_sem)
@@ -190,7 +194,12 @@
         return carry
 
     lax.fori_loop(0, 4, place_cot, 0)
-    scatter_units(buf_a, garr, ga_s, ga_r, 1, EARLY)
+
+    def cot_units(lo, count):
+        some_units(buf_a, garr, ga_s, ga_r, lo, count)
+
+    cot_units(1, COT[0])
+    next_cot = 1 + COT[0]
 
     for h in range(2):
         landed(block(h), dg_r.at[h])
@@ -259,7 +268,8 @@
         return carry
 
     lax.fori_loop(0, 4, to_owner, 0)
-    scatter_units(buf_a, garr, ga_s, ga_r, EARLY, CHIPS)
+    cot_units(next_cot, COT[1])
+    next_cot = next_cot + COT[1]
     pltpu.make_async_copy(zxs.at[z], zxr.at[z], zx_r.at[z]).start()
 
     def owner_sent():
@@ -294,6 +304,7 @@
 
     lax.fori_loop(0, 4, place_nrm, 0)
     scatter_units(buf_b, narr, na_s, na_r)
+    scatter_units(buf_a, garr, ga_s, ga_r, next_cot)
 
     down2[...] = jnp.transpose(down_t[...])
 
@@ -309,17 +320,8 @@
 
         lax.fori_loop(0, 4, group, 0)
 
-    collect(garr, ga_r)
+    collect(narr, na_r)
     load_wd.wait()
-
-    def back_down(n, carry):
-        at = pl.ds(pl.multiple_of(n * 256, 256), 256)
-        gact[:, at] = mm_t(xin[...], wd[at, :])
-        return carry
-
-    lax.fori_loop(0, 4, back_down, 0)
-
-    collect(narr, na_r)
     load_wg.wait()
     load_wu.wait()
 
@@ -327,15 +329,21 @@
         at = pl.ds(pl.multiple_of(n * 256, 256), 256)
         gate = mm(xin[...], wg[:, at])
         up = mm(xin[...], wu[:, at])
-        ga = gact[:, at]
+        gates[:, at] = gate
+        ups[:, at] = up
+        act[:, at] = (gate * jax.nn.sigmoid(gate) * up).astype(BF)
+        return carry
+
+    lax.fori_loop(0, 4, forward, 0)
+
+    def backward(n, carry):
+        at = pl.ds(pl.multiple_of(n * 256, 256), 256)
+        ga = mm_t(xin[...], wd[at, :])
+        gate = gates[:, at]
         s = jax.nn.sigmoid(gate)
-        silu = gate * s
-        act[:, at] = (silu * up).astype(BF)
-        gg[:, at] = (ga * up * s * (1.0 + gate * (1.0 - s))).astype(BF)
-        gu[:, at] = (ga * silu).astype(BF)
-        return carry
-
-    lax.fori_loop(0, 4, forward, 0)
+        gg[:, at] = (ga * ups[:, at] * s * (1.0 + gate * (1.0 - s))).astype(BF)
+        gu[:, at] = (ga * (gate * s)).astype(BF)
+        return carry
 
     def to_zin(q, rows):
         rows = rows.astype(BF)
@@ -355,22 +363,27 @@
 
         lax.fori_loop(0, 4, group, 0)
 
-    lax.fori_loop(0, 4, back_in, 0)
-    sent_units(buf_b, na_s)
-    from_zin(buf_b)
-    scatter_units(buf_b, hret, ha_s, ha_r)
-    pending.append(lambda: sent_units(buf_b, ha_s))
-
     def down_out(q, carry):
         at = pl.ds(pl.multiple_of(q * quarter, 128), quarter)
         to_zin(q, mm(act[...], wd[:, at]))
         return carry
 
+    def out_units(lo, count):
+        some_units(buf_b, eret, ea_s, ea_r, lo, count)
+
     lax.fori_loop(0, 4, down_out, 0)
+    sent_units(buf_b, na_s)
+    from_zin(buf_b)
+    out_units(1, OUT[0])
+    collect(garr, ga_r)
+    lax.fori_loop(0, 4, backward, 0)
+    lax.fori_loop(0, 4, back_in, 0)
     sent_units(buf_a, ga_s)
     from_zin(buf_a)
-    scatter_units(buf_a, eret, ea_s, ea_r)
-    pending.append(lambda: sent_units(buf_a, ea_s))
+    scatter_units(buf_a, hret, ha_s, ha_r)
+    pending.append(lambda: sent_units(buf_a, ha_s))
+    out_units(1 + OUT[0], OUT[1])
+    next_out = 1 + OUT[0] + OUT[1]
 
     def share(u):
         def pack(q, carry):
@@ -412,52 +425,52 @@
         to = (z + k) % 4
         pending.append(send(gsp.at[to], gs_all.at[tn, z], gx_s.at[k], gx_r.at[z], over_z[k]).wait_send)
     pltpu.make_async_copy(gsp.at[z], gs_all.at[tn, z], gx_r.at[z]).start()
-    for m in range(4):
+    out_units(next_out, OUT[2])
+    next_out2 = next_out + OUT[2]
+    next_out2 = next_out + OUT[2]
+    for n, k in enumerate((1, 3, 2, 0)):
+        m = (z + k) % 4
         landed(gs_all.at[tn, m], gx_r.at[m])
 
-    def gather_gs(k, carry):
-        t2 = ((tc // 4 + k // 4) % 2) * 4 + (y + k % 4) % 4
-        send(gs_all.at[tn], gs_all.at[tn], gs_s.at[k], gs_r.at[tc], (dp, t2 * 2 + c))
-        return carry
-
-    lax.fori_loop(1, 8, gather_gs, 0)
-    send(gs_all.at[tn], gs_all.at[tn], fw_s.at[tc], fw_r.at[tc], partner)
-
-    def forward_gs(k, carry):
-        t2 = ((tc // 4 + k // 4) % 2) * 4 + (y + k % 4) % 4
-        b2 = t2 * 2 + c
-        landed(gs_all.at[b2], gs_r.at[t2])
-        send(gs_all.at[b2], gs_all.at[b2], fw_s.at[t2], fw_r.at[t2], partner)
-        return carry
-
-    lax.fori_loop(1, 8, forward_gs, 0)
+        def gather_gs(i, carry):
+            t2 = ((tc // 4 + i // 4) % 2) * 4 + (y + i % 4) % 4
+            send(gs_all.at[tn, m], gs_all.at[tn, m], gs_s.at[m], gs_r.at[m, tc], (dp, t2 * 2 + c))
+            return carry
+
+        lax.fori_loop(1, 8, gather_gs, 0)
+        send(gs_all.at[tn, m], gs_all.at[tn, m], fw_s.at[m], fw_r.at[m, tc], partner)
+        out_units(next_out2 + n * OUT[3], OUT[3])
+
+    for k in (1, 3, 2, 0):
+        m = (z + k) % 4
+
+        def forward_gs(i, carry):
+            t2 = ((tc // 4 + i // 4) % 2) * 4 + (y + i % 4) % 4
+            b2 = t2 * 2 + c
+            landed(gs_all.at[b2, m], gs_r.at[m, t2])
+            send(gs_all.at[b2, m], gs_all.at[b2, m], fw_s.at[m], fw_r.at[m, t2], partner)
+            return carry
+
+        lax.fori_loop(1, 8, forward_gs, 0)
+
+        def all_gs(t, carry):
+            landed(gs_all.at[t * 2 + 1 - c, m], fw_r.at[m, t])
+            return carry
+
+        lax.fori_loop(0, 8, all_gs, 0)
+        gh = mm_t(down2[...], gs_all[:, m].reshape(256, quarter))
+        if k:
+            ghs[k] = gh.astype(BF)
+            pending.append(send(ghs.at[k], ghr.at[z], gh_s.at[k], gh_r.at[z], over_z[k]).wait_send)
 
     def gs_sent():
-        def one(k, carry):
-            landed(gs_all.at[0], gs_s.at[k])
-            return carry
-
-        lax.fori_loop(1, 8, one, 0)
-
-        def two(k, carry):
-            landed(gs_all.at[0], fw_s.at[k])
-            return carry
-
-        lax.fori_loop(0, 8, two, 0)
+        for m in range(4):
+            landed(gs_all.at[pl.ds(0, 7), 0], gs_s.at[m])
+            landed(gs_all.at[pl.ds(0, 8), 0], fw_s.at[m])
 
     pending.append(gs_sent)
-
-    def all_gs(t, carry):
-        landed(gs_all.at[t * 2 + 1 - c], fw_r.at[t])
-        return carry
-
-    lax.fori_loop(0, 8, all_gs, 0)
-    for k in (2, 1, 3, 0):
-        to = (z + k) % 4
-        gh = mm_t(down2[...], gs_all[:, to].reshape(256, quarter))
-        ghs[k] = gh.astype(BF)
-        if k:
-            pending.append(send(ghs.at[k], ghr.at[z], gh_s.at[k], gh_r.at[z], over_z[k]).wait_send)
+    scatter_units(buf_b, eret, ea_s, ea_r, next_out2 + 4 * OUT[3])
+    pending.append(lambda: sent_units(buf_b, ea_s))
 
     total = jnp.zeros((256, quarter), F32)
     for g in range(4):
@@ -507,7 +520,7 @@
         V((1024, 128), BF), V((1024, 256), BF), V((128, 1024), BF), V((256, 1024), BF),
         V((256, 256), BF), V((256, 256), BF), V((128, q), BF), V((256, q), BF),
         V(unit, BF), V(unit, BF), V(unit, BF), V(unit, BF), V(unit, BF), V(unit, BF),
-        V((256, width), BF), V((256, fe), F32), V((256, fe), BF), V((256, fe), BF), V((256, fe), BF),
+        V((256, width), BF), V((256, fe), F32), V((256, fe), F32), V((256, fe), BF), V((256, fe), BF), V((256, fe), BF),
         V((4, 256, q), BF),
         V((4, 16, 16, q), F32), V((4, 8, 16, q), BF), V((4, 8, 16, q), BF), V((4, 8, 16, q), BF),
         V((4, 8, 16, q), BF), V((4, 16, q), F32), V((4, 16, q), F32), V((16, width), F32), V((16, width), BF),
@@ -515,7 +528,7 @@
         V((4, hidden_units, 256), BF), V((4, hidden_units, 256), BF),
         dma((4,)), dma((4,)), dma((4,)), dma((4,)), dma((4,)), dma, dma((2,)), dma((4,)), dma((4,)), dma((4,)), dma((4,)), dma((4,)), dma((4,)), dma((4,)), dma((4,)), dma((4,)), dma((4,)),
         dma, dma((4,)), dma, dma((4,)), dma, dma((4,)), dma, dma((4,)),
-        dma((2,)), dma((2,)), dma((8,)), dma((8,)), dma((8,)), dma((8,)),
+        dma((2,)), dma((2,)), dma((4,)), dma((4, 8)), dma((4,)), dma((4, 8)),
     ]
     moe, gs, gh = pl.pallas_call(
         kernel,

time: 184 us -> 167 us (0.908)
  the two profiles are of different devices: /device:TPU:5 before, /device:TPU:33 now
where the time goes in v3:
time: 167 us; the launch traced here: 166 us
  Pallas kernels  165 us (99%)
    pallas_call x1, Pallas kernels, body(): pl.pallas_call(kernel, out_shape=(jax.ShapeDtypeStruct(residual.shape, BF...  163 us

profile of v3, /device:TPU:33, one launch (start us, length us, event | category | flops | bytes accessed | tf_op | source)
XLA Modules:
  0.0 165.6 jit_solution(5980717039554412954)
XLA Ops:
  0.6 163.1 %shard_map.121 = (bf16[16,3584]{1,0:T(8,128)(2,1)}, bf16[16,3584]{1,0:T(8,128)(2,1)}, bf16[576,256]{1,0:T(8,128)(2,1)}) custom-call(bf16[576,256]{1,0:T(8,128)(2,1)} %bitcast.12, bf16[448,576]{1,0:T(8,128)(2,1)} %bitcast.11, bf16[16,3584]{1,0:T(8,128)(2,1)} %res.1, bf16[3584]{0:T(1024)(128)(2,1)} %gain_in.1, bf16[16,3584]{1,0:T(8,128)(2,1)} %cot.1, ...), custom_call_target="tpu_custom_call" | custom-call | tf_op jit(solution)/shard_map/pallas_call | solution.py:533
  163.7 1.9 %shard_map.122 = (bf16[16,3584]{1,0:T(8,128)(2,1)}, bf16[16,3584]{1,0:T(8,128)(2,1)}, bf16[576,256]{1,0:T(8,128)(2,1)}) custom-call(bf16[16,3584]{1,0:T(8,128)(2,1)} %get-tuple-element.9.a, bf16[16,3584]{1,0:T(8,128)(2,1)} %get-tuple-element.10.b, bf16[576,256]{1,0:T(8,128)(2,1)} %get-tuple-element.11.c), custom_call_target="tpu_custom_call" | custom-call | tf_op jit(solution)/shard_map/pallas_call | solution.py:550

commit v4 on v3

--- a/solution.py
+++ b/solution.py
@@ -9,8 +9,8 @@
 BF = jnp.bfloat16
 F32 = jnp.float32
 CHIPS = 64
-COT = (6, 16)
-OUT = (22, 14, 10, 2)
+COT = (0, 26)
+OUT = (28, 20, 8, 1)
 ROWS = 16
 NT = (((1,), (1,)), ((), ()))
 
@@ -37,7 +37,7 @@
     xin, gates, ups, act, gg, gu, zin,
     pf, psend, prec, rs_send, rs_recv, zxs, zxr, dense_f, stream,
     acc, pax, prx, gsp, gs_all, ghs, ghr,
-    loc, ex_s, ex_r, hg_s, hg_r, dg_s, dg_r, zx_s, zx_r, gx_s, gx_r, gh_s, gh_r, ps_s, ps_r, rs_s, rs_r,
+    plane, space, loc, ex_s, ex_r, hg_s, hg_r, dg_s, dg_r, zx_s, zx_r, gx_s, gx_r, gh_s, gh_r, ps_s, ps_r, rs_s, rs_r,
     ga_s, ga_r, na_s, na_r, ha_s, ha_r, ea_s, ea_r, px_s, px_r, gs_s, gs_r, fw_s, fw_r,
 ):
     width = res.shape[1]
@@ -86,13 +86,18 @@
 
     barrier = pltpu.get_barrier_semaphore()
 
-    def greet(i, carry):
-        d2, t2 = peer(i)
-        pl.semaphore_signal(barrier, inc=1, device_id=(d2, t2 * 2 + c), device_id_type=MESH)
-        return carry
-
-    lax.fori_loop(1, CHIPS, greet, 0)
-    pl.semaphore_signal(barrier, inc=1, device_id=partner, device_id_type=MESH)
+    def on_line(dx, dy, dz):
+        x2, y2, z2 = (x + dx) % 4, (y + dy) % 4, (z + dz) % 4
+        return (x2 // 2) * 4 + z2, ((x2 % 2) * 4 + y2) * 2 + c
+
+    def signal(sem, to):
+        pl.semaphore_signal(sem, inc=1, device_id=to, device_id_type=MESH)
+
+    signal(barrier, partner)
+    for k in (1, 2, 3):
+        signal(barrier, on_line(0, 0, k))
+        signal(barrier, on_line(k, 0, 0))
+        signal(barrier, on_line(0, k, 0))
 
     lane = lax.broadcasted_iota(jnp.int32, (16, 128), 1)
     spread = jnp.where(lane % 16 == lax.broadcasted_iota(jnp.int32, (16, 128), 0), 1.0, 0.0)
@@ -104,7 +109,9 @@
     wt2[c] = lanes(wt_in[...])
     cot2[c] = cot[...]
     gain[...] = gain_in[...].reshape(1, width)
-    pl.semaphore_wait(barrier, CHIPS)
+    pl.semaphore_wait(barrier, 10)
+    for k in (1, 2, 3):
+        signal(plane, on_line(0, k, 0))
 
     ex = [
         send(key2.at[c], key2.at[c], ex_s.at[1], ex_r.at[1], partner),
@@ -120,6 +127,10 @@
     load_wg.start()
     load_wu.start()
     load_wd.start()
+
+    pl.semaphore_wait(plane, 3)
+    for k in (1, 2, 3):
+        signal(space, on_line(0, 0, k))
 
     o = lax.broadcasted_iota(jnp.int32, (256, 256), 0)
     i = lax.broadcasted_iota(jnp.int32, (256, 256), 1)
@@ -181,6 +192,48 @@
     def sent_units(src, s_sem):
         landed(src.at[pl.ds(0, CHIPS - 1)], s_sem)
 
+    for h in range(2):
+        landed(block(h), dg_r.at[h])
+
+    def turn(i):
+        return (z + i + i // 2 - i // 3 * 2) % 4
+
+    def dense(i, carry):
+        m = turn(i)
+        landed(hid.at[m], hg_r.at[m])
+        pf[m] = mm_t(jnp.transpose(hid[m]), down_t[...]).reshape(16, 16, quarter)
+
+        def pack(t, carry):
+            psend[m, t] = pf[m, 2 * t + 1 - c].astype(BF)
+            return carry
+
+        lax.fori_loop(0, 8, pack, 0)
+        send(psend.at[m], prec.at[m], ps_s.at[m], ps_r.at[m], partner)
+        return carry
+
+    lax.fori_loop(0, 4, dense, 0)
+
+    def reduce(i, carry):
+        m = turn(i)
+        landed(prec.at[m], ps_r.at[m])
+
+        def add(t, carry):
+            rs_send[m, t] = (pf[m, 2 * t + c] + prec[m, t].astype(F32)).astype(BF)
+            return carry
+
+        lax.fori_loop(0, 8, add, 0)
+
+        def out(k, carry):
+            t2 = ((tc // 4 + k // 4) % 2) * 4 + (y + k % 4) % 4
+            send(rs_send.at[m, t2], rs_recv.at[m, tc], rs_s.at[m], rs_r.at[m], (dp, t2 * 2 + c))
+            return carry
+
+        lax.fori_loop(1, 8, out, 0)
+        pltpu.make_async_copy(rs_send.at[m, tc], rs_recv.at[m, tc], rs_r.at[m]).start()
+        return carry
+
+    lax.fori_loop(0, 4, reduce, 0)
+
     for q in range(4):
         for b in range(2):
             part = cot2[b, :, q * quarter : (q + 1) * quarter]
@@ -198,50 +251,9 @@
     def cot_units(lo, count):
         some_units(buf_a, garr, ga_s, ga_r, lo, count)
 
+    pl.semaphore_wait(space, 3)
     cot_units(1, COT[0])
     next_cot = 1 + COT[0]
-
-    for h in range(2):
-        landed(block(h), dg_r.at[h])
-
-    def turn(i):
-        return (z + i + i // 2 - i // 3 * 2) % 4
-
-    def dense(i, carry):
-        m = turn(i)
-        landed(hid.at[m], hg_r.at[m])
-        pf[m] = mm_t(jnp.transpose(hid[m]), down_t[...]).reshape(16, 16, quarter)
-
-        def pack(t, carry):
-            psend[m, t] = pf[m, 2 * t + 1 - c].astype(BF)
-            return carry
-
-        lax.fori_loop(0, 8, pack, 0)
-        send(psend.at[m], prec.at[m], ps_s.at[m], ps_r.at[m], partner)
-        return carry
-
-    lax.fori_loop(0, 4, dense, 0)
-
-    def reduce(i, carry):
-        m = turn(i)
-        landed(prec.at[m], ps_r.at[m])
-
-        def add(t, carry):
-            rs_send[m, t] = (pf[m, 2 * t + c] + prec[m, t].astype(F32)).astype(BF)
-            return carry
-
-        lax.fori_loop(0, 8, add, 0)
-
-        def out(k, carry):
-            t2 = ((tc // 4 + k // 4) % 2) * 4 + (y + k % 4) % 4
-            send(rs_send.at[m, t2], rs_recv.at[m, tc], rs_s.at[m], rs_r.at[m], (dp, t2 * 2 + c))
-            return carry
-
-        lax.fori_loop(1, 8, out, 0)
-        pltpu.make_async_copy(rs_send.at[m, tc], rs_recv.at[m, tc], rs_r.at[m]).start()
-        return carry
-
-    lax.fori_loop(0, 4, reduce, 0)
 
     def sums_sent():
         def one(m, carry):
@@ -526,6 +538,7 @@
         V((4, 8, 16, q), BF), V((4, 16, q), F32), V((4, 16, q), F32), V((16, width), F32), V((16, width), BF),
         V((2, 8, 16, q), F32), V((2, 4, 16, q), F32), V((2, 4, 16, q), F32), V((4, 16, q), BF), V((16, 4, 16, q), BF),
         V((4, hidden_units, 256), BF), V((4, hidden_units, 256), BF),
+        pltpu.SemaphoreType.REGULAR, pltpu.SemaphoreType.REGULAR,
         dma((4,)), dma((4,)), dma((4,)), dma((4,)), dma((4,)), dma, dma((2,)), dma((4,)), dma((4,)), dma((4,)), dma((4,)), dma((4,)), dma((4,)), dma((4,)), dma((4,)), dma((4,)), dma((4,)),
         dma, dma((4,)), dma, dma((4,)), dma, dma((4,)), dma, dma((4,)),
         dma((2,)), dma((2,)), dma((4,)), dma((4, 8)), dma((4,)), dma((4, 8)),

time: 167 us -> 163 us (0.976)
  Pallas kernels: 165 us -> 162 us
    pallas_call x1, Pallas kernels: 163 us -> 160 us  [body(): pl.pallas_call(kernel, out_shape=(jax.ShapeDtypeStruct(residual.shape, BF...]
where the time goes in v4:
time: 163 us
  Pallas kernels  162 us (99%)
    pallas_call x1, Pallas kernels, body(): pl.pallas_call(kernel, out_shape=(jax.ShapeDtypeStruct(residual.shape, BF...  160 us

profile of v4, /device:TPU:33, one launch (start us, length us, event | category | flops | bytes accessed | tf_op | source)
XLA Modules:
  0.0 162.8 jit_solution(16505420207763964876)
XLA Ops:
  0.6 160.3 %shard_map.121 = (bf16[16,3584]{1,0:T(8,128)(2,1)}, bf16[16,3584]{1,0:T(8,128)(2,1)}, bf16[576,256]{1,0:T(8,128)(2,1)}) custom-call(bf16[576,256]{1,0:T(8,128)(2,1)} %bitcast.12, bf16[448,576]{1,0:T(8,128)(2,1)} %bitcast.11, bf16[16,3584]{1,0:T(8,128)(2,1)} %res.1, bf16[3584]{0:T(1024)(128)(2,1)} %gain_in.1, bf16[16,3584]{1,0:T(8,128)(2,1)} %cot.1, ...), custom_call_target="tpu_custom_call" | custom-call | tf_op jit(solution)/shard_map/pallas_call | solution.py:546
  160.9 1.9 %shard_map.122 = (bf16[16,3584]{1,0:T(8,128)(2,1)}, bf16[16,3584]{1,0:T(8,128)(2,1)}, bf16[576,256]{1,0:T(8,128)(2,1)}) custom-call(bf16[16,3584]{1,0:T(8,128)(2,1)} %get-tuple-element.9.a, bf16[16,3584]{1,0:T(8,128)(2,1)} %get-tuple-element.10.b, bf16[576,256]{1,0:T(8,128)(2,1)} %get-tuple-element.11.c), custom_call_target="tpu_custom_call" | custom-call | tf_op jit(solution)/shard_map/pallas_call | solution.py:563

commit v5 on v4

--- a/solution.py
+++ b/solution.py
@@ -10,7 +10,7 @@
 F32 = jnp.float32
 CHIPS = 64
 COT = (0, 26)
-OUT = (28, 20, 8, 1)
+OUT = (36, 20, 4, 0)
 ROWS = 16
 NT = (((1,), (1,)), ((), ()))
 
@@ -61,6 +61,13 @@
         z2 = (z + i + 2 * u + i // 16) % 4
         return (x2 // 2) * 4 + z2, (x2 % 2) * 4 + y2
 
+    def origin(i):
+        u = i // 4 % 4
+        x2 = (x + 3 * i) % 4
+        y2 = (y + 3 * (i + u)) % 4
+        z2 = (z + 3 * (i + 2 * u + i // 16)) % 4
+        return (x2 // 2) * 4 + z2, (x2 % 2) * 4 + y2
+
     def send(src, dst, s_sem, r_sem, device):
         copy = pltpu.make_async_remote_copy(
             src_ref=src, dst_ref=dst, send_sem=s_sem, recv_sem=r_sem,
@@ -180,14 +187,26 @@
     def some_units(src, dst, s_sem, r_sem, lo, count):
         def one(i, carry):
             d2, t2 = peer(lo + i)
-            send(src.at[d2 * 8 + t2], dst.at[chip], s_sem, r_sem.at[chip // 16], (d2, t2 * 2 + c))
+            send(src.at[d2 * 8 + t2], dst.at[lo + i], s_sem, r_sem.at[(lo + i) // 16], (d2, t2 * 2 + c))
             return carry
 
         lax.fori_loop(0, count, one, 0)
 
     def scatter_units(src, dst, s_sem, r_sem, lo=1):
+        pltpu.make_async_copy(src.at[chip], dst.at[0], r_sem.at[0]).start()
         some_units(src, dst, s_sem, r_sem, lo, CHIPS - lo)
-        pltpu.make_async_copy(src.at[chip], dst.at[chip], r_sem.at[chip // 16]).start()
+
+    def return_some(src, dst, s_sem, r_sem, lo, count):
+        def one(i, carry):
+            d2, t2 = origin(lo + i)
+            send(src.at[lo + i], dst.at[chip], s_sem, r_sem.at[chip // 16], (d2, t2 * 2 + c))
+            return carry
+
+        lax.fori_loop(0, count, one, 0)
+
+    def return_units(src, dst, s_sem, r_sem, lo=1):
+        pltpu.make_async_copy(src.at[0], dst.at[chip], r_sem.at[chip // 16]).start()
+        return_some(src, dst, s_sem, r_sem, lo, CHIPS - lo)
 
     def sent_units(src, s_sem):
         landed(src.at[pl.ds(0, CHIPS - 1)], s_sem)
@@ -381,7 +400,7 @@
         return carry
 
     def out_units(lo, count):
-        some_units(buf_b, eret, ea_s, ea_r, lo, count)
+        return_some(buf_b, eret, ea_s, ea_r, lo, count)
 
     lax.fori_loop(0, 4, down_out, 0)
     sent_units(buf_b, na_s)
@@ -392,7 +411,7 @@
     lax.fori_loop(0, 4, back_in, 0)
     sent_units(buf_a, ga_s)
     from_zin(buf_a)
-    scatter_units(buf_a, hret, ha_s, ha_r)
+    return_units(buf_a, hret, ha_s, ha_r)
     pending.append(lambda: sent_units(buf_a, ha_s))
     out_units(1 + OUT[0], OUT[1])
     next_out = 1 + OUT[0] + OUT[1]
@@ -481,7 +500,7 @@
             landed(gs_all.at[pl.ds(0, 8), 0], fw_s.at[m])
 
     pending.append(gs_sent)
-    scatter_units(buf_b, eret, ea_s, ea_r, next_out2 + 4 * OUT[3])
+    return_units(buf_b, eret, ea_s, ea_r, next_out2 + 4 * OUT[3])
     pending.append(lambda: sent_units(buf_b, ea_s))
 
     total = jnp.zeros((256, quarter), F32)

time: 163 us -> 162 us (level)
  no operation moved by 1% of the time
where the time goes in v5:
time: 162 us
  Pallas kernels  161 us (99%)
    pallas_call x1, Pallas kernels, body(): pl.pallas_call(kernel, out_shape=(jax.ShapeDtypeStruct(residual.shape, BF...  159 us

profile of v5, /device:TPU:33, one launch (start us, length us, event | category | flops | bytes accessed | tf_op | source)
XLA Modules:
  0.0 161.6 jit_solution(14549684210968513316)
XLA Ops:
  0.6 159.1 %shard_map.121 = (bf16[16,3584]{1,0:T(8,128)(2,1)}, bf16[16,3584]{1,0:T(8,128)(2,1)}, bf16[576,256]{1,0:T(8,128)(2,1)}) custom-call(bf16[576,256]{1,0:T(8,128)(2,1)} %bitcast.12, bf16[448,576]{1,0:T(8,128)(2,1)} %bitcast.11, bf16[16,3584]{1,0:T(8,128)(2,1)} %res.1, bf16[3584]{0:T(1024)(128)(2,1)} %gain_in.1, bf16[16,3584]{1,0:T(8,128)(2,1)} %cot.1, ...), custom_call_target="tpu_custom_call" | custom-call | tf_op jit(solution)/shard_map/pallas_call | solution.py:565
  159.7 1.9 %shard_map.122 = (bf16[16,3584]{1,0:T(8,128)(2,1)}, bf16[16,3584]{1,0:T(8,128)(2,1)}, bf16[576,256]{1,0:T(8,128)(2,1)}) custom-call(bf16[16,3584]{1,0:T(8,128)(2,1)} %get-tuple-element.9.a, bf16[16,3584]{1,0:T(8,128)(2,1)} %get-tuple-element.10.b, bf16[576,256]{1,0:T(8,128)(2,1)} %get-tuple-element.11.c), custom_call_target="tpu_custom_call" | custom-call | tf_op jit(solution)/shard_map/pallas_call | solution.py:582

commit v6 on v5

--- a/solution.py
+++ b/solution.py
@@ -410,8 +410,10 @@
     lax.fori_loop(0, 4, backward, 0)
     lax.fori_loop(0, 4, back_in, 0)
     sent_units(buf_a, ga_s)
-    from_zin(buf_a)
-    return_units(buf_a, hret, ha_s, ha_r)
+    for g in range(4):
+        buf_a[g * 16 : (g + 1) * 16] = mm(perm_t[...], zin[g]).astype(BF).reshape(16, ROWS, quarter)
+        return_some(buf_a, hret, ha_s, ha_r, max(g * 16, 1), 16 if g else 15)
+    pltpu.make_async_copy(buf_a.at[0], hret.at[chip], ha_r.at[chip // 16]).start()
     pending.append(lambda: sent_units(buf_a, ha_s))
     out_units(1 + OUT[0], OUT[1])
     next_out = 1 + OUT[0] + OUT[1]

time: 162 us -> 162 us (level)
  no operation moved by 1% of the time
where the time goes in v6:
time: 162 us
  Pallas kernels  161 us (99%)
    pallas_call x1, Pallas kernels, body(): pl.pallas_call(kernel, out_shape=(jax.ShapeDtypeStruct(residual.shape, BF...  159 us

profile of v6, /device:TPU:33, one launch (start us, length us, event | category | flops | bytes accessed | tf_op | source)
XLA Modules:
  0.0 161.9 jit_solution(2917430705481689125)
XLA Ops:
  0.6 159.4 %shard_map.121 = (bf16[16,3584]{1,0:T(8,128)(2,1)}, bf16[16,3584]{1,0:T(8,128)(2,1)}, bf16[576,256]{1,0:T(8,128)(2,1)}) custom-call(bf16[576,256]{1,0:T(8,128)(2,1)} %bitcast.12, bf16[448,576]{1,0:T(8,128)(2,1)} %bitcast.11, bf16[16,3584]{1,0:T(8,128)(2,1)} %res.1, bf16[3584]{0:T(1024)(128)(2,1)} %gain_in.1, bf16[16,3584]{1,0:T(8,128)(2,1)} %cot.1, ...), custom_call_target="tpu_custom_call" | custom-call | tf_op jit(solution)/shard_map/pallas_call | solution.py:567
  160.0 1.9 %shard_map.122 = (bf16[16,3584]{1,0:T(8,128)(2,1)}, bf16[16,3584]{1,0:T(8,128)(2,1)}, bf16[576,256]{1,0:T(8,128)(2,1)}) custom-call(bf16[16,3584]{1,0:T(8,128)(2,1)} %get-tuple-element.9.a, bf16[16,3584]{1,0:T(8,128)(2,1)} %get-tuple-element.10.b, bf16[576,256]{1,0:T(8,128)(2,1)} %get-tuple-element.11.c), custom_call_target="tpu_custom_call" | custom-call | tf_op jit(solution)/shard_map/pallas_call | solution.py:584
